TPU v7x, 128 devices: a whole 4x4x4 slice. The times are simulated.
128 devices in a mesh: seg: 16 (over x, z), sub: 8 (over y, core).
Axes of the slice: x: 4, y: 4, z: 4, core: 2. Of those that a mesh axis runs over, the one named last changes fastest.
Arguments:
- points: float32 [3, 524288], P(None, ('seg', 'sub')), may hold values from 0 to 1
- forces: float32 [3, 524288], P(None, ('seg', 'sub')), may hold values from -2 to 2
- near_leaf: int32 [4096, 13], P(('seg', 'sub')), may hold values from 0 to 31
- far_owner: int32 [4096, 14], P(('seg', 'sub')), may hold values from 0 to 127, all different within a row; in each aligned block of 32 rows (0 to 31, 32 to 63, ...) at most 7 rows name the same one
- far_slot: int32 [4096, 14], P(('seg', 'sub')), may hold values from 0 to 31
Outputs:
- potential: float32 [3, 524288], P(None, ('seg', 'sub'))
Inputs may be any that keep to these rules, and one draw needn't show every extreme that they name: `far_owner`: the 14 owners named by one leaf differ. Among the leaves of one device (aligned blocks of 32 rows) no owner is named more than 7 times, a bound that some block reaches.
All inputs are finite; a program needn't handle non-finite values.
Results may differ from a plain program's by a relative error of at most 0.00002.
Values sent between devices are 32-bit elements; how exact they have to be, the bound alone decides.
No kernel may reach another device: no remote copies, remote signals or barrier semaphores. Data moves between devices by JAX's collectives and lax.ppermute only.
A program may use at most 128 MiB of HBM per device.

v0:
```python
import math

import jax
import jax.numpy as jnp
from jax import lax
from jax.sharding import PartitionSpec as P

LEAF = 128


shear_term = 1.0 / (4.0 * math.pi)
couple_term = shear_term / (4.0 * (1.0 - 0.3))
radius_soft = 0.05
leaf_group = 4


def kelvinlet(targets, sources):
    offsets = targets[..., :, :, None] - sources[..., :3, None, :]
    squared = jnp.sum(offsets * offsets, axis=-3)
    inverse = lax.rsqrt(squared + radius_soft * radius_soft)
    inverse_cube = inverse * inverse * inverse
    weight = (
        shear_term - couple_term
    ) * inverse + 0.5 * shear_term * radius_soft * radius_soft * inverse_cube
    loads = sources[..., 3:, None, :]
    projected = jnp.sum(offsets * loads, axis=-3)
    coupled = couple_term * inverse_cube * projected
    return jnp.sum(weight[..., None, :, :] * loads + coupled[..., None, :, :] * offsets, axis=-1)


def leaf_sums(targets, sources):
    leaf_count = targets.shape[0]
    groups = leaf_count // leaf_group
    grouped_targets = targets.reshape(groups, leaf_group, 1, 3, LEAF)
    grouped_sources = sources.reshape(groups, leaf_group, sources.shape[1], 6, LEAF)

    def one_group(pieces):
        return jnp.sum(kelvinlet(pieces[0], pieces[1]), axis=1)

    return lax.map(one_group, (grouped_targets, grouped_sources)).reshape(leaf_count, 3, LEAF)


def per_device(points, forces, near_leaf, far_owner, far_slot):
    leaf_count = near_leaf.shape[0]
    far_count = far_owner.shape[1]
    devices = lax.axis_size(("seg", "sub"))
    blocks = jnp.concatenate(
        [points.reshape(3, leaf_count, LEAF), forces.reshape(3, leaf_count, LEAF)], 0
    ).transpose(1, 0, 2)
    targets = blocks[:, :3]
    near_part = leaf_sums(targets, blocks[near_leaf])
    flat_owner = far_owner.reshape(-1)
    flat_slot = far_slot.reshape(-1)
    capacity = max(2, (2 * leaf_count * far_count + devices - 1) // devices)
    owner_table = (flat_owner[:, None] == jnp.arange(devices, dtype=jnp.int32)[None, :]).astype(
        jnp.int32
    )
    earlier = jnp.cumsum(owner_table, axis=0) - owner_table
    rank = jnp.sum(earlier * owner_table, axis=1)
    position = flat_owner * capacity + rank
    wanted = jnp.zeros((devices * capacity,), jnp.int32).at[position].set(flat_slot)
    asked = lax.all_to_all(
        wanted.reshape(devices, capacity), ("seg", "sub"), split_axis=0, concat_axis=0, tiled=True
    )
    reply = blocks[asked]
    answers = lax.all_to_all(reply, ("seg", "sub"), split_axis=0, concat_axis=0, tiled=True)
    far_sources = answers.reshape(devices * capacity, 6, LEAF)[position]
    far_part = leaf_sums(targets, far_sources.reshape(leaf_count, far_count, 6, LEAF))
    total = near_part + far_part
    return total.transpose(1, 0, 2).reshape(3, leaf_count * LEAF)


def solution(mesh):
    in_specs = (
        P(None, ("seg", "sub")),
        P(None, ("seg", "sub")),
        P(("seg", "sub"), None),
        P(("seg", "sub"), None),
        P(("seg", "sub"), None),
    )
    out_specs = P(None, ("seg", "sub"))
    return jax.shard_map(
        per_device, mesh=mesh, in_specs=in_specs, out_specs=out_specs, check_vma=False
    )
```

profile of v0, /device:TPU:0, one launch (start us, length us, event | category | flops | bytes accessed | tf_op | source)
XLA Modules:
  0.0 173.1 jit_solution(17579423087216524134)
XLA Ops:
  7.1 11.1 %all-to-all-start = ((s32[128,1,7]{2,1,0:T(1,128)}), s32[128,1,7]{2,1,0:T(1,128)S(1)}, u32[]{:S(2)}, u32[]{:S(2)}) async-start(s32[128,1,7]{2,1,0:T(1,128)} %bitcast.19), calls=%async_computation | async-start | bytes 131072 | tf_op jit(solution)/shard_map/all_to_all | solution.py:62
  22.7 4.8 %all-to-all-done = s32[128,1,7]{2,1,0:T(1,128)S(1)} async-done(((s32[128,1,7]{2,1,0:T(1,128)}), s32[128,1,7]{2,1,0:T(1,128)S(1)}, u32[]{:S(2)}, u32[]{:S(2)}) %all-to-all-start) | async-done | bytes 3616 | tf_op jit(solution)/shard_map/all_to_all | solution.py:62
  27.7 4.0 %gather_fusion.1 = f32[896,6,128]{2,1,0:T(8,128)} fusion(f32[32,6,128]{2,1,0:T(8,128)S(1)} %maximum_bitcast_fusion, s32[1024]{0:T(1024)S(1)} %pad_clamp_fusion.1), kind=kCustom, calls=%fused_computation.1 | custom fusion | bytes 5508608 | tf_op jit(solution)/shard_map/gather | solution.py:65
  31.8 4.5 %copy.66 = f32[128,7,6,128]{3,1,2,0:T(8,128)} copy(f32[128,7,6,128]{3,2,1,0:T(8,128)} %bitcast.60) | data formatting | bytes 5505024 | tf_op jit(solution)/shard_map/gather | solution.py:65
  36.2 5.1 %all-to-all-start.1 = ((f32[128,7,6,128]{3,1,2,0:T(8,128)}), f32[128,7,6,128]{3,1,2,0:T(8,128)S(1)}, u32[]{:S(2)}, u32[]{:S(2)}) async-start(f32[128,7,6,128]{3,1,2,0:T(8,128)} %copy.66), calls=%async_computation.1 | async-start | bytes 6291456 | tf_op jit(solution)/shard_map/all_to_all | solution.py:66
  41.4 65.9 %while.20 = (s32[]{:T(128)}, f32[8,4,3,128]{3,2,1,0:T(4,128)S(1)}, f32[8,4,1,3,128]{4,3,1,2,0:T(4,128)S(1)}, f32[8,4,13,6,128]{4,3,2,1,0:T(8,128)}, s32[]{:T(128)}) while((s32[]{:T(128)}, f32[8,4,3,128]{3,2,1,0:T(4,128)S(1)}, f32[8,4,1,3,128]{4,3,1,2,0:T(4,128)S(1)}, f32[8,4,13,6,128]{4,3,2,1,0:T(8,128)}, s32[]{:T(128)}) %tuple.63), condition=%wide.region_4.5_spmd, body=%wide.region_0.4_spmd.sunk | while | flops 30669312 | bytes 28268624 | solution.py:40
  42.4 2.9 %fusion.23 = (f32[4,13,128,128]{3,2,1,0:T(8,128)S(1)}, f32[4,13,128,128]{3,2,1,0:T(8,128)S(1)}) fusion(f32[4,13,3,128]{3,2,1,0:T(4,128)S(1)} %get-tuple-element.157, f32[4,3,128]{2,1,0:T(4,128)S(1)} %dynamic-slice_bitcast_fusion.9, f32[4,13,3,128]{3,2,1,0:T(4,128)S(1)} %get-tuple-element.158), kind=kLoop, calls=%fused_computation.7.clone.1 | loop fusion | flops 11075584 | bytes 6981632 | tf_op jit(solution)/shard_map/while/body/eval_jaxpr/reduce_sum | solution.py:19
  50.7 2.9 %fusion.23 = (f32[4,13,128,128]{3,2,1,0:T(8,128)S(1)}, f32[4,13,128,128]{3,2,1,0:T(8,128)S(1)}) fusion(f32[4,13,3,128]{3,2,1,0:T(4,128)S(1)} %get-tuple-element.157, f32[4,3,128]{2,1,0:T(4,128)S(1)} %dynamic-slice_bitcast_fusion.9, f32[4,13,3,128]{3,2,1,0:T(4,128)S(1)} %get-tuple-element.158), kind=kLoop, calls=%fused_computation.7.clone.1 | loop fusion | flops 11075584 | bytes 6981632 | tf_op jit(solution)/shard_map/while/body/eval_jaxpr/reduce_sum | solution.py:19
  58.9 2.9 %fusion.23 = (f32[4,13,128,128]{3,2,1,0:T(8,128)S(1)}, f32[4,13,128,128]{3,2,1,0:T(8,128)S(1)}) fusion(f32[4,13,3,128]{3,2,1,0:T(4,128)S(1)} %get-tuple-element.157, f32[4,3,128]{2,1,0:T(4,128)S(1)} %dynamic-slice_bitcast_fusion.9, f32[4,13,3,128]{3,2,1,0:T(4,128)S(1)} %get-tuple-element.158), kind=kLoop, calls=%fused_computation.7.clone.1 | loop fusion | flops 11075584 | bytes 6981632 | tf_op jit(solution)/shard_map/while/body/eval_jaxpr/reduce_sum | solution.py:19
  67.2 2.9 %fusion.23 = (f32[4,13,128,128]{3,2,1,0:T(8,128)S(1)}, f32[4,13,128,128]{3,2,1,0:T(8,128)S(1)}) fusion(f32[4,13,3,128]{3,2,1,0:T(4,128)S(1)} %get-tuple-element.157, f32[4,3,128]{2,1,0:T(4,128)S(1)} %dynamic-slice_bitcast_fusion.9, f32[4,13,3,128]{3,2,1,0:T(4,128)S(1)} %get-tuple-element.158), kind=kLoop, calls=%fused_computation.7.clone.1 | loop fusion | flops 11075584 | bytes 6981632 | tf_op jit(solution)/shard_map/while/body/eval_jaxpr/reduce_sum | solution.py:19
  75.4 2.9 %fusion.23 = (f32[4,13,128,128]{3,2,1,0:T(8,128)S(1)}, f32[4,13,128,128]{3,2,1,0:T(8,128)S(1)}) fusion(f32[4,13,3,128]{3,2,1,0:T(4,128)S(1)} %get-tuple-element.157, f32[4,3,128]{2,1,0:T(4,128)S(1)} %dynamic-slice_bitcast_fusion.9, f32[4,13,3,128]{3,2,1,0:T(4,128)S(1)} %get-tuple-element.158), kind=kLoop, calls=%fused_computation.7.clone.1 | loop fusion | flops 11075584 | bytes 6981632 | tf_op jit(solution)/shard_map/while/body/eval_jaxpr/reduce_sum | solution.py:19
  83.6 2.9 %fusion.23 = (f32[4,13,128,128]{3,2,1,0:T(8,128)S(1)}, f32[4,13,128,128]{3,2,1,0:T(8,128)S(1)}) fusion(f32[4,13,3,128]{3,2,1,0:T(4,128)S(1)} %get-tuple-element.157, f32[4,3,128]{2,1,0:T(4,128)S(1)} %dynamic-slice_bitcast_fusion.9, f32[4,13,3,128]{3,2,1,0:T(4,128)S(1)} %get-tuple-element.158), kind=kLoop, calls=%fused_computation.7.clone.1 | loop fusion | flops 11075584 | bytes 6981632 | tf_op jit(solution)/shard_map/while/body/eval_jaxpr/reduce_sum | solution.py:19
  91.9 2.9 %fusion.23 = (f32[4,13,128,128]{3,2,1,0:T(8,128)S(1)}, f32[4,13,128,128]{3,2,1,0:T(8,128)S(1)}) fusion(f32[4,13,3,128]{3,2,1,0:T(4,128)S(1)} %get-tuple-element.157, f32[4,3,128]{2,1,0:T(4,128)S(1)} %dynamic-slice_bitcast_fusion.9, f32[4,13,3,128]{3,2,1,0:T(4,128)S(1)} %get-tuple-element.158), kind=kLoop, calls=%fused_computation.7.clone.1 | loop fusion | flops 11075584 | bytes 6981632 | tf_op jit(solution)/shard_map/while/body/eval_jaxpr/reduce_sum | solution.py:19
  100.1 2.9 %fusion.23 = (f32[4,13,128,128]{3,2,1,0:T(8,128)S(1)}, f32[4,13,128,128]{3,2,1,0:T(8,128)S(1)}) fusion(f32[4,13,3,128]{3,2,1,0:T(4,128)S(1)} %get-tuple-element.157, f32[4,3,128]{2,1,0:T(4,128)S(1)} %dynamic-slice_bitcast_fusion.9, f32[4,13,3,128]{3,2,1,0:T(4,128)S(1)} %get-tuple-element.158), kind=kLoop, calls=%fused_computation.7.clone.1 | loop fusion | flops 11075584 | bytes 6981632 | tf_op jit(solution)/shard_map/while/body/eval_jaxpr/reduce_sum | solution.py:19
  109.9 3.0 %gather_fusion.2 = f32[448,6,128]{2,1,0:T(8,128)S(1)} fusion(f32[896,6,128]{2,1,0:T(8,128)} %bitcast.61, s32[1024]{0:T(1024)S(1)} %pad_clamp_fusion), kind=kCustom, calls=%fused_computation.2 | custom fusion | bytes 2754304 | tf_op jit(solution)/shard_map/gather | solution.py:67
  112.9 59.5 %while.21 = (s32[]{:T(128)}, f32[8,4,3,128]{3,2,1,0:T(4,128)S(1)}, f32[8,4,1,3,128]{4,3,1,2,0:T(4,128)S(1)}, f32[8,4,14,6,128]{4,3,2,1,0:T(8,128)S(1)}, s32[]{:T(128)}) while((s32[]{:T(128)}, f32[8,4,3,128]{3,2,1,0:T(4,128)S(1)}, f32[8,4,1,3,128]{4,3,1,2,0:T(4,128)S(1)}, f32[8,4,14,6,128]{4,3,2,1,0:T(8,128)S(1)}, s32[]{:T(128)}) %tuple.62), condition=%wide.region_13.14_spmd, body=%wide.region_9.13_spmd.sunk | while | flops 33028608 | bytes 30439504 | solution.py:40
  113.2 3.0 %fusion.26 = (f32[4,14,128,128]{3,2,1,0:T(8,128)S(1)}, f32[4,14,128,128]{3,2,1,0:T(8,128)S(1)}) fusion(f32[4,14,3,128]{3,2,1,0:T(4,128)S(1)} %get-tuple-element.167, f32[4,3,128]{2,1,0:T(4,128)S(1)} %dynamic-slice_bitcast_fusion.11, f32[4,14,3,128]{3,2,1,0:T(4,128)S(1)} %get-tuple-element.168), kind=kLoop, calls=%fused_computation.21.clone.1 | loop fusion | flops 11927552 | bytes 7518208 | tf_op jit(solution)/shard_map/while/body/eval_jaxpr/reduce_sum | solution.py:19
  120.6 3.0 %fusion.26 = (f32[4,14,128,128]{3,2,1,0:T(8,128)S(1)}, f32[4,14,128,128]{3,2,1,0:T(8,128)S(1)}) fusion(f32[4,14,3,128]{3,2,1,0:T(4,128)S(1)} %get-tuple-element.167, f32[4,3,128]{2,1,0:T(4,128)S(1)} %dynamic-slice_bitcast_fusion.11, f32[4,14,3,128]{3,2,1,0:T(4,128)S(1)} %get-tuple-element.168), kind=kLoop, calls=%fused_computation.21.clone.1 | loop fusion | flops 11927552 | bytes 7518208 | tf_op jit(solution)/shard_map/while/body/eval_jaxpr/reduce_sum | solution.py:19
  128.0 3.0 %fusion.26 = (f32[4,14,128,128]{3,2,1,0:T(8,128)S(1)}, f32[4,14,128,128]{3,2,1,0:T(8,128)S(1)}) fusion(f32[4,14,3,128]{3,2,1,0:T(4,128)S(1)} %get-tuple-element.167, f32[4,3,128]{2,1,0:T(4,128)S(1)} %dynamic-slice_bitcast_fusion.11, f32[4,14,3,128]{3,2,1,0:T(4,128)S(1)} %get-tuple-element.168), kind=kLoop, calls=%fused_computation.21.clone.1 | loop fusion | flops 11927552 | bytes 7518208 | tf_op jit(solution)/shard_map/while/body/eval_jaxpr/reduce_sum | solution.py:19
  135.4 3.0 %fusion.26 = (f32[4,14,128,128]{3,2,1,0:T(8,128)S(1)}, f32[4,14,128,128]{3,2,1,0:T(8,128)S(1)}) fusion(f32[4,14,3,128]{3,2,1,0:T(4,128)S(1)} %get-tuple-element.167, f32[4,3,128]{2,1,0:T(4,128)S(1)} %dynamic-slice_bitcast_fusion.11, f32[4,14,3,128]{3,2,1,0:T(4,128)S(1)} %get-tuple-element.168), kind=kLoop, calls=%fused_computation.21.clone.1 | loop fusion | flops 11927552 | bytes 7518208 | tf_op jit(solution)/shard_map/while/body/eval_jaxpr/reduce_sum | solution.py:19
  142.9 3.0 %fusion.26 = (f32[4,14,128,128]{3,2,1,0:T(8,128)S(1)}, f32[4,14,128,128]{3,2,1,0:T(8,128)S(1)}) fusion(f32[4,14,3,128]{3,2,1,0:T(4,128)S(1)} %get-tuple-element.167, f32[4,3,128]{2,1,0:T(4,128)S(1)} %dynamic-slice_bitcast_fusion.11, f32[4,14,3,128]{3,2,1,0:T(4,128)S(1)} %get-tuple-element.168), kind=kLoop, calls=%fused_computation.21.clone.1 | loop fusion | flops 11927552 | bytes 7518208 | tf_op jit(solution)/shard_map/while/body/eval_jaxpr/reduce_sum | solution.py:19
  150.3 3.0 %fusion.26 = (f32[4,14,128,128]{3,2,1,0:T(8,128)S(1)}, f32[4,14,128,128]{3,2,1,0:T(8,128)S(1)}) fusion(f32[4,14,3,128]{3,2,1,0:T(4,128)S(1)} %get-tuple-element.167, f32[4,3,128]{2,1,0:T(4,128)S(1)} %dynamic-slice_bitcast_fusion.11, f32[4,14,3,128]{3,2,1,0:T(4,128)S(1)} %get-tuple-element.168), kind=kLoop, calls=%fused_computation.21.clone.1 | loop fusion | flops 11927552 | bytes 7518208 | tf_op jit(solution)/shard_map/while/body/eval_jaxpr/reduce_sum | solution.py:19
  157.7 3.0 %fusion.26 = (f32[4,14,128,128]{3,2,1,0:T(8,128)S(1)}, f32[4,14,128,128]{3,2,1,0:T(8,128)S(1)}) fusion(f32[4,14,3,128]{3,2,1,0:T(4,128)S(1)} %get-tuple-element.167, f32[4,3,128]{2,1,0:T(4,128)S(1)} %dynamic-slice_bitcast_fusion.11, f32[4,14,3,128]{3,2,1,0:T(4,128)S(1)} %get-tuple-element.168), kind=kLoop, calls=%fused_computation.21.clone.1 | loop fusion | flops 11927552 | bytes 7518208 | tf_op jit(solution)/shard_map/while/body/eval_jaxpr/reduce_sum | solution.py:19
  165.1 3.0 %fusion.26 = (f32[4,14,128,128]{3,2,1,0:T(8,128)S(1)}, f32[4,14,128,128]{3,2,1,0:T(8,128)S(1)}) fusion(f32[4,14,3,128]{3,2,1,0:T(4,128)S(1)} %get-tuple-element.167, f32[4,3,128]{2,1,0:T(4,128)S(1)} %dynamic-slice_bitcast_fusion.11, f32[4,14,3,128]{3,2,1,0:T(4,128)S(1)} %get-tuple-element.168), kind=kLoop, calls=%fused_computation.21.clone.1 | loop fusion | flops 11927552 | bytes 7518208 | tf_op jit(solution)/shard_map/while/body/eval_jaxpr/reduce_sum | solution.py:19
  (137 shorter events, 91.5 us)
Async XLA Ops:
  7.1 20.4 %all-to-all-start = ((s32[128,1,7]{2,1,0:T(1,128)}), s32[128,1,7]{2,1,0:T(1,128)S(1)}, u32[]{:S(2)}, u32[]{:S(2)}) async-start(s32[128,1,7]{2,1,0:T(1,128)} %bitcast.19), calls=%async_computation | async-start | bytes 131072 | tf_op jit(solution)/shard_map/all_to_all | solution.py:62
  20.1 11.7 %copy-start = (f32[32,6,128]{2,1,0:T(8,128)}, f32[32,6,128]{2,1,0:T(8,128)S(1)}, u32[]{:S(2)}) copy-start(f32[32,6,128]{2,1,0:T(8,128)S(1)} %maximum_bitcast_fusion) | copy-start | bytes 294916
  36.2 5.2 %slice-start = ((f32[32,6,128]{2,1,0:T(8,128)}), f32[32,3,128]{2,1,0:T(4,128)S(1)}, s32[]{:S(2)}) async-start(f32[32,6,128]{2,1,0:T(8,128)} %copy-done), calls=%async_computation.2 | async-start | bytes 131072 | tf_op jit(solution)/shard_map/slice | solution.py:50
  36.2 71.1 %all-to-all-start.1 = ((f32[128,7,6,128]{3,1,2,0:T(8,128)}), f32[128,7,6,128]{3,1,2,0:T(8,128)S(1)}, u32[]{:S(2)}, u32[]{:S(2)}) async-start(f32[128,7,6,128]{3,1,2,0:T(8,128)} %copy.66), calls=%async_computation.1 | async-start | bytes 6291456 | tf_op jit(solution)/shard_map/all_to_all | solution.py:66
where the time goes:
time: 174 us; the launch traced here: 173 us
  other arithmetic  118 us (68%)
  local copies, waits for them, and re-layouts  32.3 us (19%)
  starting transfers between devices  16.3 us (9%)
  waiting for transfers between devices  4.81 us (3%)
    reduce_sum x16, other arithmetic, kelvinlet(): squared = jnp.sum(offsets * offsets, axis=-3)  47.8 us
    reduce_sum x16, other arithmetic, one_group(): return jnp.sum(kelvinlet(pieces[0], pieces[1]), axis=1)  41.6 us
    add x16, other arithmetic, kelvinlet(): (shear_term - couple_term) * inverse  26 us
    all_to_all x1, starting transfers between devices, per_device(): lax.all_to_all(wanted.reshape(devices, capacity), ('seg', 'sub'), split_a...  11.1 us
    gather x2, local copies, waits for them, and re-layouts, per_device(): reply = blocks[asked]  8.49 us
    squeeze x16, local copies, waits for them, and re-layouts, leaf_sums(): lax.map(one_group, (grouped_targets, grouped_sources))  7.83 us
    all_to_all x1, starting transfers between devices, per_device(): lax.all_to_all(reply, ('seg', 'sub'), split_axis=0, concat_axis=0, tiled=...  5.13 us
    all_to_all x1, waiting for transfers between devices, per_device(): lax.all_to_all(wanted.reshape(devices, capacity), ('seg', 'sub'), split_a...  4.81 us
  transfers between devices with their start and end apart: 2, of which 1 were waited for; matrix products, arithmetic and copies ran while one was open for 40% of the time, Pallas kernels for 0%

commit v1 on v0

v1 whole, which is shorter than its diff:
```python
import functools
import math

import jax
import jax.numpy as jnp
from jax import lax
from jax.experimental import pallas as pl
from jax.experimental.pallas import tpu as pltpu
from jax.sharding import PartitionSpec as P

A = 1.0 / (4.0 * math.pi)
B = A / (4.0 * (1.0 - 0.3))
E = 0.05
C1 = A - B
C2 = A * E * E / 2
K2 = C1 / C2
WSC = C1 * math.sqrt(K2)
QK = B / C1 * K2
KE = K2 * E * E
CAP = 7
PER = 48
f32 = jnp.float32
bf16 = jnp.bfloat16
PA=['y0','y1','y2','f0','f1','f2','y0','y0','y0','y1','y1','y1','y2','y2','y2',None]
PB=[None]*6+['f0','f1','f2','f0','f1','f2','f0','f1','f2',None]
PC=[None,'f0','f1','f2']*2
PD=[None,'y0','y1','y2']*2
ROWS=PA+PB+PC+PD
NEED={n:[i for i,r in enumerate(ROWS) if r==n] for n in ('y0','y1','y2','f0','f1','f2')}
NAMES=('y0','y1','y2','f0','f1','f2')

def split3(v):
    a=v.astype(bf16); r=v-a.astype(f32)
    b=r.astype(bf16); r=r-b.astype(f32)
    return a,b,r.astype(bf16)

def lin_coef(table,row):
    co=[0.0]*3
    if table==0:
        if row<3: co[row]=-2.0*K2
        return co
    i=table-1
    if 6<=row<15:
        a,b=divmod(row-6,3)
        if i==b: co[a]-=2.0*K2
        if i==a: co[b]-=QK
        if a==b: co[i]-=QK
    return co

def const_rows(vals):
    r=lax.broadcasted_iota(jnp.int32,(8,128),0)
    v=jnp.full((8,128),vals[0],f32)
    for k in range(1,8): v=jnp.where(r==k,vals[k],v)
    return v

def kern(n_src, near, idx_ref, tgt_ref, *rest):
    if near:
        y_src,f_src,out_ref,w_ref,cen_ref,st_ref,co_ref,lhs_ref=rest
        def row(c,s):
            return y_src[c,pl.ds(s,1),:] if c<3 else f_src[c-3,pl.ds(s,1),:]
    else:
        src_ref,out_ref,w_ref,cen_ref,st_ref,co_ref,lhs_ref=rest
        def row(c,s): return src_ref[pl.ds(s+c,1),:]
    n=tgt_ref.shape[1]
    for g in range(0,n,8):
        for c in range(3):
            v=tgt_ref[c,g:g+8,:]
            cen_ref[c,g:g+8,:]=jnp.broadcast_to(jnp.mean(v,axis=1,keepdims=True),(8,128))
    for T in range(4):
        for H in range(2):
            for a in range(3):
                co_ref[(T*2+H)*3+a]=const_rows([lin_coef(T,8*H+r)[a] for r in range(8)])
    def init(l,_):
        st_ref[l]=jnp.ones((48,128),f32)
        if near:
            fill(l,l)
        return 0
    def fill(l,s):
        for c,nm in enumerate(NAMES):
            v=row(c,s)
            for i in NEED[nm]: st_ref[l,i:i+1,:]=v
    lax.fori_loop(0,st_ref.shape[0],init,0)
    sub=lax.broadcasted_iota(jnp.int32,(8,128),0)
    r16=lax.broadcasted_iota(jnp.int32,(16,512),0); l16=lax.broadcasted_iota(jnp.int32,(16,512),1)//128
    wone=jnp.where((r16<12)&(r16%4==l16),1.0,0.0).astype(bf16)
    for sl in range(2):
        w_ref[sl,96:112,:]=wone
        w_ref[sl,112:128,:]=jnp.zeros((16,512),bf16)
    def prep_w(t,slot):
        x=[jnp.broadcast_to(tgt_ref[c,pl.ds(t,1),:]-cen_ref[c,pl.ds(t,1),:],(8,128)) for c in range(3)]
        xx=K2*(x[0]*x[0]+x[1]*x[1]+x[2]*x[2])
        xj=QK*jnp.where(sub==3,x[0],jnp.where(sub==4,x[1],jnp.where(sub==5,x[2],0.0)))
        for T in range(4):
            hs=[]
            for H in range(2):
                v=None
                for a in range(3):
                    if any(lin_coef(T,8*H+r)[a]!=0 for r in range(8)):
                        w=co_ref[(T*2+H)*3+a]*x[a]
                        v=w if v is None else v+w
                if v is None: v=jnp.zeros((8,128),f32)
                if T==0 and H==1: v=jnp.where(sub==7,xx,v)
                if T>0 and H==0: v=v+x[T-1]*xj+jnp.where(sub==2+T,xx,0.0)
                hs.append(v)
            b1,b2,b3=split3(jnp.concatenate(hs,0))
            ls=slice(128*T,128*T+128)
            for blk,b in enumerate((b1,b2,b3,b1,b2,b1)):
                w_ref[slot,16*blk:16*blk+16,ls]=b
    def prep_leaf(t,k,slot,cenA,cenD,cen):
        s=idx_ref[t,k]
        if near: l=s
        else:
            l=k; fill(l,s)
        y=[jnp.broadcast_to(row(c,s),(8,128))-cen[c] for c in range(3)]
        f=[jnp.broadcast_to(row(3+c,s),(8,128)) for c in range(3)]
        Y=K2*(y[0]*y[0]+y[1]*y[1]+y[2]*y[2])+jnp.where(sub%4==0,KE,KE+1.0)
        yf=QK*(y[0]*f[0]+y[1]*f[1]+y[2]*f[2])
        t48=st_ref[l]
        V=(t48[0:16]-cenA)*t48[16:32]
        C=t48[32:40]*Y+yf*(t48[40:48]-cenD)
        C=jnp.where(sub%4==0,Y,C)
        a,b,c=split3(V)
        p=C.astype(bf16).astype(f32); r=C-p
        o=r.astype(bf16).astype(f32); r=r-o
        cc=jnp.concatenate([jnp.where(sub<4,p,o),jnp.where(sub<4,r,0.0)],0).astype(bf16)
        at=jnp.concatenate([a,a,a,b,b,c,cc,cc],0)
        lhs_ref[slot,128*k:128*k+128,:]=jnp.transpose(at)
    def cens(t):
        cen=[jnp.broadcast_to(cen_ref[c,pl.ds(t,1),:],(8,128)) for c in range(3)]
        def pat(rows):
            v=jnp.zeros((8,128),f32)
            for c in range(3):
                for k,nm in enumerate(rows):
                    if nm=='y%d'%c: v=jnp.where(sub==k,cen[c],v)
            return v
        return jnp.concatenate([pat(PA[:8]),pat(PA[8:])],0),pat(PD),cen
    def prep_all(t,slot):
        prep_w(t,slot)
        cs=cens(t)
        for k in range(n_src): prep_leaf(t,k,slot,*cs)
    def step(t,slot):
        tn=jnp.minimum(t+1,n-1); ns=1-slot
        T=lax.dot_general(lhs_ref[slot],w_ref[slot],(((1,),(0,)),((),())),preferred_element_type=f32)
        cs=cens(tn)
        acc=[jnp.zeros((8,128),f32) for _ in range(3)]
        prep_w(tn,ns)
        for k in range(n_src):
            for rr in range(16*k,16*k+16):
                S=T[8*rr:8*rr+8,0:128]
                h=lax.rsqrt(S); e=h*h*h
                acc=[acc[c]+e*T[8*rr:8*rr+8,128*(c+1):128*(c+2)] for c in range(3)]
            prep_leaf(tn,k,ns,*cs)
        for c in range(3):
            out_ref[c,pl.ds(t,1),:]=jnp.sum(acc[c],axis=0,keepdims=True)*WSC
    prep_all(0,0)
    def body(i,_):
        step(2*i,0); step(2*i+1,1)
        return 0
    lax.fori_loop(0,n//2,body,0)

def call(n_src, near, idx, tgt, *src):
    n=tgt.shape[1]
    vm=pl.BlockSpec(memory_space=pltpu.VMEM)
    return pl.pallas_call(functools.partial(kern,n_src,near), out_shape=jax.ShapeDtypeStruct((3,n,128),f32),
            in_specs=[pl.BlockSpec(memory_space=pltpu.SMEM)]+[vm]*(1+len(src)),
            out_specs=vm,
            scratch_shapes=[pltpu.VMEM((2,128,512),bf16),pltpu.VMEM((3,n,128),f32),pltpu.VMEM((n if near else n_src,48,128),f32),
              pltpu.VMEM((24,8,128),f32),pltpu.VMEM((2,n_src*128,128),bf16)],
            name="near" if near else "far",
            cost_estimate=pl.CostEstimate(flops=20000000000,bytes_accessed=1000000,transcendentals=0),
            compiler_params=pltpu.CompilerParams(vmem_limit_bytes=40<<20))(idx,tgt,*src)


def request_kernel(owner_ref, slot_ref, want_ref, base_ref):
    rows, far = owner_ref.shape
    lane = lax.broadcasted_iota(jnp.int32, (rows, 128), 1)
    named = jnp.zeros((rows, 128), f32)
    slots = jnp.zeros((rows, 128), f32)
    hits = []
    for k in range(far):
        hit = jnp.where(owner_ref[:, k:k+1] == lane, 1.0, 0.0)
        hits.append(hit)
        named = named + hit
        slots = slots + hit * slot_ref[:, k:k+1].astype(f32)
    before = lax.broadcasted_iota(jnp.int32, (rows, rows), 1) < lax.broadcasted_iota(jnp.int32, (rows, rows), 0)
    rank = jnp.dot(before.astype(bf16), named.astype(bf16), preferred_element_type=f32)
    wanted = [jnp.sum(jnp.where(rank == r, slots, 0.0), axis=0, keepdims=True) for r in range(CAP)]
    wanted = jnp.concatenate(wanted + [jnp.zeros((128 - CAP, 128), f32)], 0)
    want_ref[...] = jnp.transpose(wanted).astype(jnp.int32)
    base = jnp.zeros((rows, 128), jnp.int32)
    for k in range(far):
        mine = jnp.sum(hits[k] * rank, axis=1, keepdims=True).astype(jnp.int32) * 6 + owner_ref[:, k:k+1] * PER
        base = jnp.where(lane == k, mine, base)
    base_ref[...] = base[:, :far]


def reply_kernel(ask_ref, y_ref, f_ref, out_ref):
    def one(p, _):
        for r in range(CAP):
            s = ask_ref[p, r]
            for c in range(6):
                v = y_ref[c, pl.ds(s, 1), :] if c < 3 else f_ref[c - 3, pl.ds(s, 1), :]
                out_ref[pl.ds(p * PER + 6 * r + c, 1), :] = v
        return 0
    lax.fori_loop(0, ask_ref.shape[0], one, 0)


def per_device(points, forces, near_leaf, far_owner, far_slot):
    n = near_leaf.shape[0]
    devices = lax.axis_size(("seg", "sub"))
    y = points.reshape(3, n, 128)
    f = forces.reshape(3, n, 128)
    vm = pl.BlockSpec(memory_space=pltpu.VMEM)
    sm = pl.BlockSpec(memory_space=pltpu.SMEM)
    want, base = pl.pallas_call(
        request_kernel,
        out_shape=(jax.ShapeDtypeStruct((devices, 128), jnp.int32), jax.ShapeDtypeStruct(far_owner.shape, jnp.int32)),
        in_specs=[vm, vm], out_specs=(vm, vm), name="requests",
    )(far_owner, far_slot)
    asked = lax.all_to_all(want.reshape(devices, 1, 128), ("seg", "sub"), split_axis=0, concat_axis=0, tiled=True)
    reply = pl.pallas_call(
        reply_kernel,
        out_shape=jax.ShapeDtypeStruct((devices * PER, 128), f32),
        in_specs=[sm, vm, vm], out_specs=vm, name="replies",
        compiler_params=pltpu.CompilerParams(vmem_limit_bytes=32 << 20),
    )(asked.reshape(devices, 128), y, f)
    answers = lax.all_to_all(reply.reshape(devices, PER, 128), ("seg", "sub"), split_axis=0, concat_axis=0, tiled=True)
    near = call(near_leaf.shape[1], True, near_leaf, y, y, f)
    far = call(far_owner.shape[1], False, base, y, answers.reshape(devices * PER, 128))
    return (near + far).reshape(3, n * 128)


def solution(mesh):
    split = P(None, ("seg", "sub"))
    rows = P(("seg", "sub"), None)
    return jax.shard_map(
        per_device, mesh=mesh, in_specs=(split, split, rows, rows, rows), out_specs=split, check_vma=False
    )
```

time: 174 us -> 101 us (0.58)
  other arithmetic: 118 us -> 0.01 us
  Pallas kernels: 0 us -> 49.6 us
  local copies, waits for them, and re-layouts: 32.3 us -> 4.38 us
  waiting for transfers between devices: 4.81 us -> 30.7 us
    reduce_sum x33 -> x0, other arithmetic: 89.6 us -> none  [the longest x16 47.8 us: kelvinlet(): squared = jnp.sum(offsets * offsets, axis=-3)]
    pallas_call x0 -> x4, Pallas kernels: none -> 49.6 us  [the longest x2 40.1 us: call(): pl.pallas_call(functools.partial(kern, n_src, near), out_shape=jax.ShapeD...]
    add x17 -> x0, other arithmetic: 26 us -> none  [the longest x16 26 us: kelvinlet(): (shear_term - couple_term) * inverse]
    all_to_all x2, waiting for transfers between devices: 4.81 us -> 30.7 us  [the longest x1 22.4 us: per_device(): lax.all_to_all(reply.reshape(devices, PER, 128), ('seg', 'sub'), split_ax...]
    gather x4 -> x0, local copies, waits for them, and re-layouts: 14 us -> none  [the longest x2 8.49 us: per_device(): reply = blocks[asked]]
    squeeze x16 -> x0, local copies, waits for them, and re-layouts: 7.83 us -> none  [leaf_sums(): lax.map(one_group, (grouped_targets, grouped_sources))]
    scatter x1 -> x0, local copies, waits for them, and re-layouts: 2.92 us -> none  [per_device(): jnp.zeros((devices * capacity,), jnp.int32).at[position].set(flat_slot)]
    reshape x2 -> x1, local copies, waits for them, and re-layouts: 2.67 us -> 0.88 us  [per_device(): f = forces.reshape(3, n, 128)]
  transfers between devices with their start and end apart: 2 -> 2, of which waited for: 1 -> 2; matrix products, arithmetic and copies ran while one was open for 40% -> 1% of each run, Pallas kernels for 0% -> 19%
where the time goes in v1:
time: 101 us
  Pallas kernels  49.6 us (49%)
  waiting for transfers between devices  30.7 us (30%)
  starting transfers between devices  16 us (16%)
  local copies, waits for them, and re-layouts  4.38 us (4%)
    pallas_call x2, Pallas kernels, call(): pl.pallas_call(functools.partial(kern, n_src, near), out_shape=jax.ShapeD...  40.1 us
    all_to_all x1, waiting for transfers between devices, per_device(): lax.all_to_all(reply.reshape(devices, PER, 128), ('seg', 'sub'), split_ax...  22.4 us
    all_to_all x1, starting transfers between devices, per_device(): lax.all_to_all(want.reshape(devices, 1, 128), ('seg', 'sub'), split_axis=...  11.1 us
    all_to_all x1, waiting for transfers between devices, per_device(): lax.all_to_all(want.reshape(devices, 1, 128), ('seg', 'sub'), split_axis=...  8.35 us
    pallas_call x1, Pallas kernels, per_device(): pl.pallas_call(reply_kernel, out_shape=jax.ShapeDtypeStruct((devices * PE...  6.69 us
    all_to_all x1, starting transfers between devices, per_device(): lax.all_to_all(reply.reshape(devices, PER, 128), ('seg', 'sub'), split_ax...  4.81 us
    unnamed x8, local copies, waits for them, and re-layouts  3.5 us
    pallas_call x1, Pallas kernels, per_device(): pl.pallas_call(request_kernel, out_shape=(jax.ShapeDtypeStruct((devices,...  2.74 us
  transfers between devices with their start and end apart: 2, of which 2 were waited for; matrix products, arithmetic and copies ran while one was open for 1% of the time, Pallas kernels for 19%

profile of v1, /device:TPU:0, one launch (start us, length us, event | category | flops | bytes accessed | tf_op | source)
XLA Modules:
  0.0 100.7 jit_solution(8377996289197895051)
XLA Ops:
  0.0 1.4 %copy.10.owner_ref = s32[32,14]{1,0:T(8,128)} copy(s32[32,14]{0,1:T(8,128)} %param.8) | data formatting | bytes 3584 | tf_op args[3]
  1.4 1.4 %copy.11.slot_ref = s32[32,14]{1,0:T(8,128)} copy(s32[32,14]{0,1:T(8,128)} %param.9) | data formatting | bytes 3584 | tf_op args[4]
  2.7 2.7 %requests.1 = (s32[128,128]{1,0:T(8,128)}, s32[32,14]{1,0:T(8,128)}) custom-call(s32[32,14]{1,0:T(8,128)} %copy.10.owner_ref, s32[32,14]{1,0:T(8,128)} %copy.11.slot_ref), custom_call_target="tpu_custom_call" | custom-call | tf_op jit(solution)/shard_map/requests/pallas_call | solution.py:215
  5.5 11.1 %all-to-all-start = ((s32[128,1,128]{2,1,0:T(1,128)}), s32[128,1,128]{2,1,0:T(1,128)S(1)}, u32[]{:S(2)}, u32[]{:S(2)}) async-start(s32[128,1,128]{2,1,0:T(1,128)} %bitcast.21), calls=%async_computation | async-start | bytes 131072 | tf_op jit(solution)/shard_map/all_to_all | solution.py:220
  16.6 0.9 copy_bitcast_fusion.1
  17.5 8.4 %all-to-all-done = s32[128,1,128]{2,1,0:T(1,128)S(1)} async-done(((s32[128,1,128]{2,1,0:T(1,128)}), s32[128,1,128]{2,1,0:T(1,128)S(1)}, u32[]{:S(2)}, u32[]{:S(2)}) %all-to-all-start) | async-done | bytes 65568 | tf_op jit(solution)/shard_map/all_to_all | solution.py:220
  25.9 6.7 %replies.1 = f32[6144,128]{1,0:T(8,128)} custom-call(s32[128,128]{1,0:T(8,128)S(1)} %bitcast.18, f32[3,32,128]{2,1,0:T(8,128)S(1)} %get-tuple-element.10.tgt_ref.rest_0_.y_ref, f32[3,32,128]{2,1,0:T(8,128)S(1)} %get-tuple-element.9.rest_1_.f_ref), custom_call_target="tpu_custom_call" | custom-call | tf_op jit(solution)/shard_map/replies/pallas_call | solution.py:221
  32.6 0.0 copy-start.1
  32.6 4.8 %all-to-all-start.1 = ((f32[128,48,128]{2,1,0:T(8,128)}), f32[128,48,128]{2,1,0:T(8,128)S(1)}, u32[]{:S(2)}, u32[]{:S(2)}) async-start(f32[128,48,128]{2,1,0:T(8,128)} %bitcast.3), calls=%async_computation.1 | async-start | bytes 6291456 | tf_op jit(solution)/shard_map/all_to_all | solution.py:227
  37.4 0.0 copy-done.1
  37.4 0.1 copy.9.idx_ref
  37.5 0.0 copy-start
  37.5 19.2 %near.1 = f32[3,32,128]{2,1,0:T(8,128)S(1)} custom-call(s32[32,13]{1,0:T(8,128)S(1)} %copy.9.idx_ref, f32[3,32,128]{2,1,0:T(8,128)S(1)} %get-tuple-element.10.tgt_ref.rest_0_.y_ref, f32[3,32,128]{2,1,0:T(8,128)S(1)} %get-tuple-element.10.tgt_ref.rest_0_.y_ref, f32[3,32,128]{2,1,0:T(8,128)S(1)} %get-tuple-element.9.rest_1_.f_ref), custom_call_target="tpu_custom_call" | custom-call | flops 20000000000 | bytes 1000000 | tf_op jit(solution)/shard_map/near/pallas_call | solution.py:164
  56.7 22.4 %all-to-all-done.1 = f32[128,48,128]{2,1,0:T(8,128)S(1)} async-done(((f32[128,48,128]{2,1,0:T(8,128)}), f32[128,48,128]{2,1,0:T(8,128)S(1)}, u32[]{:S(2)}, u32[]{:S(2)}) %all-to-all-start.1) | async-done | bytes 3145760 | tf_op jit(solution)/shard_map/all_to_all | solution.py:227
  79.1 0.0 copy-done
  79.1 20.9 %far.1 = f32[3,32,128]{2,1,0:T(8,128)S(1)} custom-call(s32[32,14]{1,0:T(8,128)S(1)} %copy-done, f32[3,32,128]{2,1,0:T(8,128)S(1)} %get-tuple-element.10.tgt_ref.rest_0_.y_ref, f32[6144,128]{1,0:T(8,128)S(1)} %bitcast.17), custom_call_target="tpu_custom_call" | custom-call | flops 20000000000 | bytes 1000000 | tf_op jit(solution)/shard_map/far/pallas_call | solution.py:164
  100.0 0.7 copy.19
  (1 shorter events, 0.0 us)
Async XLA Ops:
  5.5 20.4 %all-to-all-start = ((s32[128,1,128]{2,1,0:T(1,128)}), s32[128,1,128]{2,1,0:T(1,128)S(1)}, u32[]{:S(2)}, u32[]{:S(2)}) async-start(s32[128,1,128]{2,1,0:T(1,128)} %bitcast.21), calls=%async_computation | async-start | bytes 131072 | tf_op jit(solution)/shard_map/all_to_all | solution.py:220
  32.6 4.8 %copy-start.1 = (s32[32,13]{0,1:T(8,128)S(1)}, s32[32,13]{0,1:T(8,128)}, u32[]{:S(2)}) copy-start(s32[32,13]{0,1:T(8,128)} %param.7) | copy-start | bytes 4996
  32.6 46.5 %all-to-all-start.1 = ((f32[128,48,128]{2,1,0:T(8,128)}), f32[128,48,128]{2,1,0:T(8,128)S(1)}, u32[]{:S(2)}, u32[]{:S(2)}) async-start(f32[128,48,128]{2,1,0:T(8,128)} %bitcast.3), calls=%async_computation.1 | async-start | bytes 6291456 | tf_op jit(solution)/shard_map/all_to_all | solution.py:227
  37.5 41.6 %copy-start = (s32[32,14]{1,0:T(8,128)S(1)}, s32[32,14]{1,0:T(8,128)}, u32[]{:S(2)}) copy-start(s32[32,14]{1,0:T(8,128)} %get-tuple-element.7.idx_ref) | copy-start | bytes 5380

commit v2 on v0

v2 whole, which is shorter than its diff:
```python
import functools
import math

import jax
import jax.numpy as jnp
from jax import lax
from jax.experimental import pallas as pl
from jax.experimental.pallas import tpu as pltpu
from jax.sharding import PartitionSpec as P

A = 1.0 / (4.0 * math.pi)
B = A / (4.0 * (1.0 - 0.3))
E = 0.05
C1 = A - B
C2 = A * E * E / 2
K2 = C1 / C2
WSC = C1 * math.sqrt(K2)
QK = B / C1 * K2
KE = K2 * E * E
CAP = 56
FIRST = 28
PER_A = 6 * FIRST
PER_B = 6 * (CAP - FIRST)
UNIT = 7
f32 = jnp.float32
bf16 = jnp.bfloat16
PA=['y0','y1','y2','f0','f1','f2','y0','y0','y0','y1','y1','y1','y2','y2','y2',None]
PB=[None]*6+['f0','f1','f2','f0','f1','f2','f0','f1','f2',None]
PC=[None,'f0','f1','f2']*2
PD=[None,'y0','y1','y2']*2
ROWS=PA+PB+PC+PD
NEED={n:[i for i,r in enumerate(ROWS) if r==n] for n in ('y0','y1','y2','f0','f1','f2')}
NAMES=('y0','y1','y2','f0','f1','f2')

def split3(v):
    a=v.astype(bf16); r=v-a.astype(f32)
    b=r.astype(bf16); r=r-b.astype(f32)
    return a,b,r.astype(bf16)

def lin_coef(table,row):
    co=[0.0]*3
    if table==0:
        if row<3: co[row]=-2.0*K2
        return co
    i=table-1
    if 6<=row<15:
        a,b=divmod(row-6,3)
        if i==b: co[a]-=2.0*K2
        if i==a: co[b]-=QK
        if a==b: co[i]-=QK
    return co

def const_rows(vals):
    r=lax.broadcasted_iota(jnp.int32,(8,128),0)
    v=jnp.full((8,128),vals[0],f32)
    for k in range(1,8): v=jnp.where(r==k,vals[k],v)
    return v

def pair_kernel(mode, n_src, *refs):
    near = mode == "near"
    w_ref, cen_ref, st_ref, co_ref, lhs_ref, order_ref = refs[-6:]
    out_ref = refs[-7]
    if near:
        idx_ref, _, y_ref, f_ref = refs[:4]
    elif mode == "first":
        idx_ref, top_ref, y_ref, part_ref, a_ref = refs[:5]
    else:
        idx_ref, top_ref, y_ref, part_ref, a_ref, b_ref = refs[:6]
    n = y_ref.shape[1] // 128

    def lanes(s):
        return pl.ds(pl.multiple_of(s * 128, 128), 128)

    def fetch(s):
        if near:
            return [y_ref[c:c+1, lanes(s)] for c in range(3)] + [f_ref[c:c+1, lanes(s)] for c in range(3)]
        last = a_ref.shape[0] - 6
        if mode == "first":
            s = jnp.minimum(s, last)
            return [a_ref[pl.ds(s + c, 1), :] for c in range(6)]
        late = s > last
        sa = jnp.where(late, 0, s)
        sb = jnp.where(late, s - a_ref.shape[0], 0)
        return [jnp.where(late, b_ref[pl.ds(sb + c, 1), :], a_ref[pl.ds(sa + c, 1), :]) for c in range(6)]

    for t in range(n):
        v = y_ref[:, 128*t:128*t+128]
        cen_ref[t, 0:3, :] = jnp.broadcast_to(jnp.mean(v, axis=1, keepdims=True), (3, 128))
    for T in range(4):
        for H in range(2):
            for a in range(3):
                co_ref[(T*2+H)*3+a] = const_rows([lin_coef(T, 8*H+r)[a] for r in range(8)])

    def fill(l, rows):
        for c, nm in enumerate(NAMES):
            for i in NEED[nm]:
                st_ref[l, i:i+1, :] = rows[c]

    def init(l, _):
        st_ref[l] = jnp.ones((48, 128), f32)
        if near:
            fill(l, fetch(l))
        return 0
    lax.fori_loop(0, st_ref.shape[0], init, 0)

    sub = lax.broadcasted_iota(jnp.int32, (8, 128), 0)
    r16 = lax.broadcasted_iota(jnp.int32, (16, 512), 0)
    l16 = lax.broadcasted_iota(jnp.int32, (16, 512), 1) // 128
    wone = jnp.where((r16 < 12) & (r16 % 4 == l16), 1.0, 0.0).astype(bf16)
    for sl in range(2):
        w_ref[sl, 96:112, :] = wone
        w_ref[sl, 112:128, :] = jnp.zeros((16, 512), bf16)

    if near:
        count = n
    else:
        out_ref[...] = part_ref[...]

        def sort(u, count):
            ready = top_ref[u % 2, u // 2] < FIRST
            order_ref[count] = u
            return count + jnp.where(ready == (mode == "first"), 1, 0)
        count = lax.fori_loop(0, 2 * n, sort, 0)

    def place(i):
        if near:
            t = jnp.minimum(i, n - 1)
            return t, lambda k: idx_ref[k, t]
        u = order_ref[jnp.maximum(jnp.minimum(i, count - 1), 0)]
        t = u // 2
        return t, lambda k: idx_ref[(u % 2) * UNIT + k, t]

    def prep_w(t, slot):
        x = [jnp.broadcast_to(y_ref[c:c+1, lanes(t)] - cen_ref[t, c:c+1, :], (8, 128)) for c in range(3)]
        xx = K2*(x[0]*x[0]+x[1]*x[1]+x[2]*x[2])
        xj = QK*jnp.where(sub == 3, x[0], jnp.where(sub == 4, x[1], jnp.where(sub == 5, x[2], 0.0)))
        for T in range(4):
            hs = []
            for H in range(2):
                v = None
                for a in range(3):
                    if any(lin_coef(T, 8*H+r)[a] != 0 for r in range(8)):
                        w = co_ref[(T*2+H)*3+a]*x[a]
                        v = w if v is None else v+w
                if v is None:
                    v = jnp.zeros((8, 128), f32)
                if T == 0 and H == 1:
                    v = jnp.where(sub == 7, xx, v)
                if T > 0 and H == 0:
                    v = v+x[T-1]*xj+jnp.where(sub == 2+T, xx, 0.0)
                hs.append(v)
            b1, b2, b3 = split3(jnp.concatenate(hs, 0))
            ls = slice(128*T, 128*T+128)
            for blk, b in enumerate((b1, b2, b3, b1, b2, b1)):
                w_ref[slot, 16*blk:16*blk+16, ls] = b

    def prep_leaf(s, k, slot, cenA, cenD, cen):
        rows = fetch(s)
        if near:
            l = s
        else:
            l = k
            fill(l, rows)
        y = [jnp.broadcast_to(rows[c], (8, 128))-cen[c] for c in range(3)]
        f = [jnp.broadcast_to(rows[3+c], (8, 128)) for c in range(3)]
        Y = K2*(y[0]*y[0]+y[1]*y[1]+y[2]*y[2])+jnp.where(sub % 4 == 0, KE, KE+1.0)
        yf = QK*(y[0]*f[0]+y[1]*f[1]+y[2]*f[2])
        t48 = st_ref[l]
        V = (t48[0:16]-cenA)*t48[16:32]
        C = t48[32:40]*Y+yf*(t48[40:48]-cenD)
        C = jnp.where(sub % 4 == 0, Y, C)
        a, b, c = split3(V)
        p = C.astype(bf16).astype(f32)
        r = C-p
        o = r.astype(bf16).astype(f32)
        r = r-o
        cc = jnp.concatenate([jnp.where(sub < 4, p, o), jnp.where(sub < 4, r, 0.0)], 0).astype(bf16)
        at = jnp.concatenate([a, a, a, b, b, c, cc, cc], 0)
        lhs_ref[slot, 128*k:128*k+128, :] = jnp.transpose(at)

    def cens(t):
        cen = [jnp.broadcast_to(cen_ref[t, c:c+1, :], (8, 128)) for c in range(3)]

        def pat(rows):
            v = jnp.zeros((8, 128), f32)
            for c in range(3):
                for k, nm in enumerate(rows):
                    if nm == "y%d" % c:
                        v = jnp.where(sub == k, cen[c], v)
            return v
        return jnp.concatenate([pat(PA[:8]), pat(PA[8:])], 0), pat(PD), cen

    def prep_all(i, slot):
        t, src = place(i)
        prep_w(t, slot)
        cs = cens(t)
        for k in range(n_src):
            prep_leaf(src(k), k, slot, *cs)

    def step(i, slot):
        t, _ = place(i)
        tn, src = place(i + 1)
        ns = 1-slot
        T = lax.dot_general(lhs_ref[slot], w_ref[slot], (((1,), (0,)), ((), ())), preferred_element_type=f32)
        cs = cens(tn)
        acc = [jnp.zeros((8, 128), f32) for _ in range(3)]
        prep_w(tn, ns)
        for k in range(n_src):
            for rr in range(16*k, 16*k+16):
                S = T[8*rr:8*rr+8, 0:128]
                h = lax.rsqrt(S)
                e = h*h*h
                acc = [acc[c]+e*T[8*rr:8*rr+8, 128*(c+1):128*(c+2)] for c in range(3)]
            prep_leaf(src(k), k, ns, *cs)
        for c in range(3):
            total = jnp.sum(acc[c], axis=0, keepdims=True)*WSC
            if near:
                out_ref[c:c+1, lanes(t)] = total
            else:
                out_ref[c:c+1, lanes(t)] += jnp.where(i < count, total, 0.0)

    prep_all(0, 0)

    def body(i, _):
        for j in range(4):
            step(4*i+j, j % 2)
        return 0
    lax.fori_loop(0, (count + 3)//4, body, 0)


VM = pl.BlockSpec(memory_space=pltpu.VMEM)
SM = pl.BlockSpec(memory_space=pltpu.SMEM)


def pairs(mode, n_src, scalars, arrays):
    n = arrays[0].shape[1] // 128
    return pl.pallas_call(
        functools.partial(pair_kernel, mode, n_src),
        out_shape=jax.ShapeDtypeStruct((3, n*128), f32),
        in_specs=[SM]*len(scalars)+[VM]*len(arrays), out_specs=VM,
        scratch_shapes=[
            pltpu.VMEM((2, 128, 512), bf16), pltpu.VMEM((n, 8, 128), f32),
            pltpu.VMEM((n if mode == "near" else n_src, 48, 128), f32), pltpu.VMEM((24, 8, 128), f32),
            pltpu.VMEM((2, n_src*128, 128), bf16), pltpu.SMEM((2*n+1,), jnp.int32)],
        name=mode, cost_estimate=pl.CostEstimate(flops=COST[mode], bytes_accessed=1000000, transcendentals=0),
        compiler_params=pltpu.CompilerParams(vmem_limit_bytes=40 << 20),
    )(*scalars, *arrays)


COST = {"near": 20000000000, "first": 16000000000, "rest": 6000000000}


def request_kernel(owner_ref, slot_ref, want_ref, base_ref, top_ref):
    far, rows = owner_ref.shape
    groups = want_ref.shape[0]
    my_y, my_core = lax.axis_index("y"), lax.axis_index("core")
    group = lax.broadcasted_iota(jnp.int32, (groups, rows), 0)
    hits = [jnp.where(lax.shift_right_logical(owner_ref[k:k+1, :], 3) == group, 1.0, 0.0) for k in range(far)]
    named = hits[0]
    for k in range(1, far):
        named = named + hits[k]
    before = lax.broadcasted_iota(jnp.int32, (rows, rows), 0) < lax.broadcasted_iota(jnp.int32, (rows, rows), 1)
    rank = jnp.dot(named.astype(bf16), before.astype(f32).astype(bf16), preferred_element_type=f32)
    place = lax.broadcasted_iota(jnp.int32, (128, rows), 0)
    want = jnp.zeros((groups, 128), f32)
    mine = []
    for k in range(far):
        own = jnp.sum(hits[k]*rank, axis=0, keepdims=True).astype(jnp.int32)
        rank = rank + hits[k]
        mine.append(own)
        o = owner_ref[k:k+1, :]
        dy = (lax.shift_right_logical(o, 1) - my_y) & 3
        dc = (o - my_core) & 1
        value = (dy*64 + dc*32 + slot_ref[k:k+1, :]).astype(f32)
        at = jnp.where(place == own, value, 0.0)
        want = want + lax.dot_general(hits[k].astype(bf16), at.astype(bf16), (((1,), (1,)), ((), ())),
                                      preferred_element_type=f32)
    want_ref[...] = want.astype(jnp.int32)
    base = []
    for k in range(far):
        asked = lax.shift_right_logical(owner_ref[k:k+1, :], 3)
        late = groups*PER_A + asked*PER_B + (mine[k]-FIRST)*6
        base.append(jnp.where(mine[k] >= FIRST, late, asked*PER_A + mine[k]*6))
    order = []
    for k in range(far):
        p = jnp.zeros((1, rows), jnp.int32)
        for j in range(far):
            if j != k:
                p = p + jnp.where((mine[j] < mine[k]) if j > k else (mine[j] <= mine[k]), 1, 0)
        order.append(p)
    for p in range(far):
        b = jnp.zeros((1, rows), jnp.int32)
        m = jnp.zeros((1, rows), jnp.int32)
        for k in range(far):
            b = b + jnp.where(order[k] == p, base[k], 0)
            if p % UNIT == UNIT-1:
                m = m + jnp.where(order[k] == p, mine[k], 0)
        base_ref[p:p+1, :] = b
        if p % UNIT == UNIT-1:
            top_ref[p//UNIT:p//UNIT+1, :] = m


def pack_kernel(y_ref, f_ref, after_ref, out_ref):
    for t in range(y_ref.shape[1] // 128):
        out_ref[8*t:8*t+3, :] = y_ref[:, 128*t:128*t+128]
        out_ref[8*t+3:8*t+6, :] = f_ref[:, 128*t:128*t+128]
        out_ref[8*t+6:8*t+8, :] = jnp.zeros((2, 128), f32)


def reply_kernel(ranks, *refs):
    ask_ref, *tables = refs[:5]
    out_ref, table_ref = refs[-2:]
    rows = tables[0].shape[0]
    for i, ref in enumerate(tables):
        table_ref[rows*i:rows*i+rows, :] = ref[...]

    def one(p, _):
        for q, r in enumerate(ranks):
            tile = table_ref[pl.ds(pl.multiple_of(ask_ref[p, r] * 8, 8), 8), :]
            out_ref[p, 6*q:6*q+6, :] = tile[0:6]
        return 0
    lax.fori_loop(0, out_ref.shape[0], one, 0)


def per_device(points, forces, near_leaf, far_owner, far_slot):
    n, near_count = near_leaf.shape
    far_count = far_owner.shape[1]
    groups = lax.axis_size("seg")
    i32 = jnp.int32
    want, base, top = pl.pallas_call(
        request_kernel,
        out_shape=(jax.ShapeDtypeStruct((groups, 128), i32), jax.ShapeDtypeStruct((far_count, n), i32),
                   jax.ShapeDtypeStruct((far_count//UNIT, n), i32)),
        in_specs=[VM, VM], out_specs=(VM, VM, VM), name="requests",
    )(far_owner.T, far_slot.T)

    def send(values):
        return lax.all_to_all(values, "seg", split_axis=0, concat_axis=0, tiled=True)
    asked = send(want.reshape(groups, 1, 128)).reshape(groups, 128)

    own = pl.pallas_call(
        pack_kernel, out_shape=jax.ShapeDtypeStruct((8*n, 128), f32), in_specs=[VM, VM, VM], out_specs=VM, name="pack",
    )(points, forces, want)
    chip = jnp.concatenate([own, lax.ppermute(own, "core", [(0, 1), (1, 0)])], 0)
    tables = [chip] + [lax.ppermute(chip, "y", [(i, (i - d) % 4) for i in range(4)]) for d in (1, 2, 3)]

    def answer(ranks, *after):
        reply = pl.pallas_call(
            functools.partial(reply_kernel, ranks),
            out_shape=jax.ShapeDtypeStruct((groups, 6*len(ranks), 128), f32),
            in_specs=[SM] + [VM]*(4 + len(after)), out_specs=VM,
            scratch_shapes=[pltpu.VMEM((64*n, 128), f32)], name="replies",
            compiler_params=pltpu.CompilerParams(vmem_limit_bytes=32 << 20),
        )(asked, *tables, *after)
        return reply, send(reply).reshape(-1, 128)
    reply_a, answers_a = answer(range(0, FIRST))
    near = pairs("near", near_count, (near_leaf.T, asked), (points, forces))
    reply_b, answers_b = answer(range(FIRST, CAP), near)
    first = pairs("first", UNIT, (base, top), (points, near, answers_a))
    return pairs("rest", UNIT, (base, top), (points, first, answers_a, answers_b))


def solution(mesh):
    grid = jax.sharding.Mesh(mesh.devices.reshape(mesh.devices.shape[0], -1, 2), ("seg", "y", "core"))
    every = ("seg", "y", "core")
    split = P(None, every)
    rows = P(every, None)
    return jax.shard_map(
        per_device, mesh=grid, in_specs=(split, split, rows, rows, rows), out_specs=split, check_vma=False
    )
```

time: 174 us -> 87.4 us (0.50)
  other arithmetic: 118 us -> 0.92 us
  Pallas kernels: 0 us -> 51.3 us
  local copies, waits for them, and re-layouts: 32.3 us -> 0.02 us
  blocking collectives: 0 us -> 15.4 us
  waiting for transfers between devices: 4.81 us -> 1.98 us
    reduce_sum x33 -> x0, other arithmetic: 89.6 us -> none  [the longest x16 47.8 us: kelvinlet(): squared = jnp.sum(offsets * offsets, axis=-3)]
    pallas_call x0 -> x7, Pallas kernels: none -> 51.3 us  [the longest x3 43.1 us: pairs(): pl.pallas_call(functools.partial(pair_kernel, mode, n_src), out_shape=jax...]
    add x17 -> x0, other arithmetic: 26 us -> none  [the longest x16 26 us: kelvinlet(): (shear_term - couple_term) * inverse]
    all_to_all x0 -> x1, blocking collectives: none -> 15.4 us  [send(): lax.all_to_all(values, 'seg', split_axis=0, concat_axis=0, tiled=True)]
    gather x4 -> x0, local copies, waits for them, and re-layouts: 14 us -> none  [the longest x2 8.49 us: per_device(): reply = blocks[asked]]
    squeeze x16 -> x0, local copies, waits for them, and re-layouts: 7.83 us -> none  [leaf_sums(): lax.map(one_group, (grouped_targets, grouped_sources))]
    ppermute x0 -> x4, starting transfers between devices: none -> 5.98 us  [the longest x3 5.98 us: per_device(): lax.ppermute(chip, 'y', [(i, (i - d) % 4) for i in range(4)])]
    all_to_all x2, starting transfers between devices: 16.3 us -> 10.9 us  [send(): lax.all_to_all(values, 'seg', split_axis=0, concat_axis=0, tiled=True)]
  transfers between devices with their start and end apart: 2 -> 6, of which waited for: 1 -> 3; matrix products, arithmetic and copies ran while one was open for 40% -> 0% of each run, Pallas kernels for 0% -> 45%
where the time goes in v2:
time: 87.4 us; the launch traced here: 86.5 us
  Pallas kernels  51.3 us (59%)
  starting transfers between devices  16.9 us (19%)
  blocking collectives  15.4 us (18%)
  waiting for transfers between devices  1.98 us (2%)
  other arithmetic  0.92 us (1%)
    pallas_call x3, Pallas kernels, pairs(): pl.pallas_call(functools.partial(pair_kernel, mode, n_src), out_shape=jax...  43.1 us
    all_to_all x1, blocking collectives, send(): lax.all_to_all(values, 'seg', split_axis=0, concat_axis=0, tiled=True)  15.4 us
    all_to_all x2, starting transfers between devices, send(): lax.all_to_all(values, 'seg', split_axis=0, concat_axis=0, tiled=True)  10.9 us
    ppermute x3, starting transfers between devices, per_device(): lax.ppermute(chip, 'y', [(i, (i - d) % 4) for i in range(4)])  5.98 us
    pallas_call x2, Pallas kernels, answer(): pl.pallas_call(functools.partial(reply_kernel, ranks), out_shape=jax.Shap...  4.77 us
    pallas_call x1, Pallas kernels, per_device(): pl.pallas_call(request_kernel, out_shape=(jax.ShapeDtypeStruct((groups, 1...  1.86 us
  transfers between devices with their start and end apart: 6, of which 3 were waited for; matrix products, arithmetic and copies ran while one was open for 0% of the time, Pallas kernels for 45%

profile of v2, /device:TPU:0, one launch (start us, length us, event | category | flops | bytes accessed | tf_op | source)
XLA Modules:
  0.0 86.5 jit_solution(14282860366594526460)
XLA Ops:
  0.0 1.9 %requests.1 = (s32[16,128]{1,0:T(8,128)}, s32[14,32]{1,0:T(8,128)}, s32[2,32]{1,0:T(2,128)}) custom-call(s32[14,32]{1,0:T(8,128)} %bitcast.17, s32[14,32]{1,0:T(8,128)} %bitcast.18), custom_call_target="tpu_custom_call" | custom-call | tf_op jit(solution)/shard_map/requests/pallas_call | solution.py:330
  1.9 1.6 %pack.1 = f32[256,128]{1,0:T(8,128)} custom-call(f32[3,4096]{1,0:T(4,128)} %refs_2_.5, f32[3,4096]{1,0:T(4,128)} %f_ref.1, s32[16,128]{1,0:T(8,128)} %get-tuple-element.10.after_ref), custom_call_target="tpu_custom_call" | custom-call | tf_op jit(solution)/shard_map/pack/pallas_call | solution.py:341
  3.4 0.0 collective-permute-start
  3.4 1.6 %collective-permute-done = f32[256,128]{1,0:T(8,128)S(1)} collective-permute-done((f32[256,128]{1,0:T(8,128)}, f32[256,128]{1,0:T(8,128)S(1)}, u32[]{:S(2)}, u32[]{:S(2)}) %collective-permute-start) | collective-permute-done | bytes 131104 | tf_op jit(solution)/shard_map/ppermute | solution.py:344
  5.0 0.9 %pad_maximum_fusion.refs_1_ = f32[512,128]{1,0:T(8,128)S(1)} fusion(f32[256,128]{1,0:T(8,128)S(1)} %collective-permute-done, f32[256,128]{1,0:T(8,128)} %pack.1), kind=kLoop, calls=%fused_computation | loop fusion | flops 65536 | bytes 524288 | tf_op jit(solution)/shard_map/concatenate | solution.py:344
  5.9 1.7 %collective-permute-start.3 = (f32[512,128]{1,0:T(8,128)S(1)}, f32[512,128]{1,0:T(8,128)S(1)}, u32[]{:S(2)}, u32[]{:S(2)}) collective-permute-start(f32[512,128]{1,0:T(8,128)S(1)} %pad_maximum_fusion.refs_1_), channel_id=1, source_target_pairs={{0,2},{2,4},{4,6},{6,0},{1,3},{3,5},{5,7},{7,1},{8,10},{10,12},{12... | collective-permute-start | bytes 786440 | tf_op jit(solution)/shard_map/ppermute | solution.py:345
  7.6 2.9 %collective-permute-start.2 = (f32[512,128]{1,0:T(8,128)S(1)}, f32[512,128]{1,0:T(8,128)S(1)}, u32[]{:S(2)}, u32[]{:S(2)}) collective-permute-start(f32[512,128]{1,0:T(8,128)S(1)} %pad_maximum_fusion.refs_1_), channel_id=1, source_target_pairs={{0,4},{2,6},{4,0},{6,2},{1,5},{3,7},{5,1},{7,3},{8,12},{10,14},{12... | collective-permute-start | bytes 786440 | tf_op jit(solution)/shard_map/ppermute | solution.py:345
  10.5 1.3 %collective-permute-start.1 = (f32[512,128]{1,0:T(8,128)S(1)}, f32[512,128]{1,0:T(8,128)S(1)}, u32[]{:S(2)}, u32[]{:S(2)}) collective-permute-start(f32[512,128]{1,0:T(8,128)S(1)} %pad_maximum_fusion.refs_1_), channel_id=1, source_target_pairs={{0,6},{2,0},{4,2},{6,4},{1,7},{3,1},{5,3},{7,5},{8,14},{10,8},{12,... | collective-permute-start | bytes 786440 | tf_op jit(solution)/shard_map/ppermute | solution.py:345
  11.9 15.4 %all_to_all.15 = s32[16,1,128]{2,1,0:T(1,128)S(1)} all-to-all(s32[16,1,128]{2,1,0:T(1,128)} %bitcast.16), channel_id=1, replica_groups=mesh['seg'=16,'y'=4,'core'=2] {'seg'}, dimensions={0} | all-to-all | bytes 16384 | tf_op jit(solution)/shard_map/all_to_all | solution.py:338
  27.2 0.0 collective-permute-done.3.refs_4_
  27.2 0.0 collective-permute-done.2.refs_3_
  27.2 0.0 collective-permute-done.1.refs_2_
  27.3 2.4 %replies.2 = f32[16,168,128]{2,1,0:T(8,128)} custom-call(s32[16,128]{1,0:T(8,128)S(1)} %bitcast.12, f32[512,128]{1,0:T(8,128)S(1)} %pad_maximum_fusion.refs_1_, f32[512,128]{1,0:T(8,128)S(1)} %collective-permute-done.1.refs_2_, f32[512,128]{1,0:T(8,128)S(1)} %collective-permute-done.2.refs_3_, f32[512,128]{1,0:T(8,128)S(1)} %collective-permute-done.3.refs_4_), custom_call_target="tpu_custom_call" | custom-call | tf_op jit(solution)/shard_map/replies/pallas_call | solution.py:348
  29.6 3.8 %all-to-all-start.1 = ((f32[16,168,128]{2,1,0:T(8,128)}), f32[16,168,128]{2,1,0:T(8,128)S(1)}, u32[]{:S(2)}, u32[]{:S(2)}) async-start(f32[16,168,128]{2,1,0:T(8,128)} %replies.2), calls=%async_computation.1 | async-start | bytes 2752512 | tf_op jit(solution)/shard_map/all_to_all | solution.py:338
  33.5 0.0 copy-done
  33.5 0.0 copy-done.1
  33.5 0.0 copy-done.2
  33.5 17.5 %near.1.refs_3_.refs_5_ = f32[3,4096]{1,0:T(4,128)S(1)} custom-call(s32[13,32]{1,0:T(8,128)S(1)} %bitcast.15, s32[16,128]{1,0:T(8,128)S(1)} %bitcast.13, f32[3,4096]{1,0:T(4,128)S(1)} %copy-done.1, f32[3,4096]{1,0:T(4,128)S(1)} %copy-done), custom_call_target="tpu_custom_call" | custom-call | flops 20000000000 | bytes 1000000 | tf_op jit(solution)/shard_map/near/pallas_call | solution.py:237
  51.0 2.4 %replies.3 = f32[16,168,128]{2,1,0:T(8,128)} custom-call(s32[16,128]{1,0:T(8,128)S(1)} %bitcast.14, f32[512,128]{1,0:T(8,128)S(1)} %pad_maximum_fusion.refs_1_, f32[512,128]{1,0:T(8,128)S(1)} %collective-permute-done.1.refs_2_, f32[512,128]{1,0:T(8,128)S(1)} %collective-permute-done.2.refs_3_, f32[512,128]{1,0:T(8,128)S(1)} %collective-permute-done.3.refs_4_, ...), custom_call_target="tpu_custom_call" | custom-call | tf_op jit(solution)/shard_map/replies/pallas_call | solution.py:348
  53.4 0.2 all-to-all-done.1
  53.6 7.1 %all-to-all-start.2 = ((f32[16,168,128]{2,1,0:T(8,128)}), f32[16,168,128]{2,1,0:T(8,128)S(1)}, u32[]{:S(2)}, u32[]{:S(2)}) async-start(f32[16,168,128]{2,1,0:T(8,128)} %replies.3), calls=%async_computation.2 | async-start | bytes 2752512 | tf_op jit(solution)/shard_map/all_to_all | solution.py:338
  60.7 19.1 %first.1.refs_3_ = f32[3,4096]{1,0:T(4,128)S(1)} custom-call(s32[14,32]{1,0:T(8,128)S(1)} %copy-done.3, s32[2,32]{1,0:T(2,128)S(1)} %copy-done.4, f32[3,4096]{1,0:T(4,128)S(1)} %copy-done.1, f32[3,4096]{1,0:T(4,128)S(1)} %near.1.refs_3_.refs_5_, f32[2688,128]{1,0:T(8,128)S(1)} %bitcast.9), custom_call_target="tpu_custom_call" | custom-call | flops 16000000000 | bytes 1000000 | tf_op jit(solution)/shard_map/first/pallas_call | solution.py:237
  79.8 0.2 all-to-all-done.2
  80.0 6.5 %rest.1 = f32[3,4096]{1,0:T(4,128)} custom-call(s32[14,32]{1,0:T(8,128)S(1)} %copy-done.3, s32[2,32]{1,0:T(2,128)S(1)} %copy-done.4, f32[3,4096]{1,0:T(4,128)S(1)} %copy-done.1, f32[3,4096]{1,0:T(4,128)S(1)} %first.1.refs_3_, f32[2688,128]{1,0:T(8,128)S(1)} %bitcast.10, f32[2688,128]{1,0:T(8,128)S(1)} %bitcast.11), custom_call_target="tpu_custom_call" | custom-call | flops 6000000000 | bytes 1000000 | tf_op jit(solution)/shard_map/rest/pallas_call | solution.py:237
  (7 shorter events, 0.0 us)
Async XLA Ops:
  3.4 1.6 %collective-permute-start = (f32[256,128]{1,0:T(8,128)}, f32[256,128]{1,0:T(8,128)S(1)}, u32[]{:S(2)}, u32[]{:S(2)}) collective-permute-start(f32[256,128]{1,0:T(8,128)} %pack.1), channel_id=1, source_target_pairs={{0,1},{1,0},{2,3},{3,2},{4,5},{5,4},{6,7},{7,6},{8,9},{9,8},{10,11... | collective-permute-start | bytes 393224 | tf_op jit(solution)/shard_map/ppermute | solution.py:344
  5.9 21.3 %collective-permute-start.3 = (f32[512,128]{1,0:T(8,128)S(1)}, f32[512,128]{1,0:T(8,128)S(1)}, u32[]{:S(2)}, u32[]{:S(2)}) collective-permute-start(f32[512,128]{1,0:T(8,128)S(1)} %pad_maximum_fusion.refs_1_), channel_id=1, source_target_pairs={{0,2},{2,4},{4,6},{6,0},{1,3},{3,5},{5,7},{7,1},{8,10},{10,12},{12... | collective-permute-start | bytes 786440 | tf_op jit(solution)/shard_map/ppermute | solution.py:345
  7.6 19.6 %collective-permute-start.2 = (f32[512,128]{1,0:T(8,128)S(1)}, f32[512,128]{1,0:T(8,128)S(1)}, u32[]{:S(2)}, u32[]{:S(2)}) collective-permute-start(f32[512,128]{1,0:T(8,128)S(1)} %pad_maximum_fusion.refs_1_), channel_id=1, source_target_pairs={{0,4},{2,6},{4,0},{6,2},{1,5},{3,7},{5,1},{7,3},{8,12},{10,14},{12... | collective-permute-start | bytes 786440 | tf_op jit(solution)/shard_map/ppermute | solution.py:345
  10.5 16.7 %collective-permute-start.1 = (f32[512,128]{1,0:T(8,128)S(1)}, f32[512,128]{1,0:T(8,128)S(1)}, u32[]{:S(2)}, u32[]{:S(2)}) collective-permute-start(f32[512,128]{1,0:T(8,128)S(1)} %pad_maximum_fusion.refs_1_), channel_id=1, source_target_pairs={{0,6},{2,0},{4,2},{6,4},{1,7},{3,1},{5,3},{7,5},{8,14},{10,8},{12,... | collective-permute-start | bytes 786440 | tf_op jit(solution)/shard_map/ppermute | solution.py:345
  29.6 3.9 %copy-start = (f32[3,4096]{1,0:T(4,128)S(1)}, f32[3,4096]{1,0:T(4,128)}, u32[]{:S(2)}) copy-start(f32[3,4096]{1,0:T(4,128)} %f_ref.1) | copy-start | bytes 147460
  29.6 3.9 %copy-start.1 = (f32[3,4096]{1,0:T(4,128)S(1)}, f32[3,4096]{1,0:T(4,128)}, u32[]{:S(2)}) copy-start(f32[3,4096]{1,0:T(4,128)} %refs_2_.5) | copy-start | bytes 147460
  29.6 3.9 %copy-start.2 = (s32[32,13]{0,1:T(8,128)S(1)}, s32[32,13]{0,1:T(8,128)}, u32[]{:S(2)}) copy-start(s32[32,13]{0,1:T(8,128)} %param.7) | copy-start | bytes 4996
  29.6 24.0 %all-to-all-start.1 = ((f32[16,168,128]{2,1,0:T(8,128)}), f32[16,168,128]{2,1,0:T(8,128)S(1)}, u32[]{:S(2)}, u32[]{:S(2)}) async-start(f32[16,168,128]{2,1,0:T(8,128)} %replies.2), calls=%async_computation.1 | async-start | bytes 2752512 | tf_op jit(solution)/shard_map/all_to_all | solution.py:338
  53.4 7.3 %copy-start.3 = (s32[14,32]{1,0:T(8,128)S(1)}, s32[14,32]{1,0:T(8,128)}, u32[]{:S(2)}) copy-start(s32[14,32]{1,0:T(8,128)} %get-tuple-element.8.refs_0_) | copy-start | bytes 5380
  53.4 7.3 %copy-start.4 = (s32[2,32]{1,0:T(2,128)S(1)}, s32[2,32]{1,0:T(2,128)}, u32[]{:S(2)}) copy-start(s32[2,32]{1,0:T(2,128)} %get-tuple-element.9.refs_1_) | copy-start | bytes 772
  53.6 26.4 %all-to-all-start.2 = ((f32[16,168,128]{2,1,0:T(8,128)}), f32[16,168,128]{2,1,0:T(8,128)S(1)}, u32[]{:S(2)}, u32[]{:S(2)}) async-start(f32[16,168,128]{2,1,0:T(8,128)} %replies.3), calls=%async_computation.2 | async-start | bytes 2752512 | tf_op jit(solution)/shard_map/all_to_all | solution.py:338

commit v3 on v2

--- a/solution.py
+++ b/solution.py
@@ -58,14 +58,14 @@
 
 def pair_kernel(mode, n_src, *refs):
     near = mode == "near"
-    w_ref, cen_ref, st_ref, co_ref, lhs_ref, order_ref = refs[-6:]
-    out_ref = refs[-7]
+    w_ref, cen_ref, st_ref, co_ref, lhs_ref = refs[-5:]
+    out_ref = refs[-6]
     if near:
         idx_ref, _, y_ref, f_ref = refs[:4]
     elif mode == "first":
-        idx_ref, top_ref, y_ref, part_ref, a_ref = refs[:5]
+        idx_ref, y_ref, part_ref, a_ref = refs[:4]
     else:
-        idx_ref, top_ref, y_ref, part_ref, a_ref, b_ref = refs[:6]
+        idx_ref, y_ref, part_ref, a_ref, b_ref = refs[:5]
     n = y_ref.shape[1] // 128
 
     def lanes(s):
@@ -116,19 +116,19 @@
     else:
         out_ref[...] = part_ref[...]
 
-        def sort(u, count):
-            ready = top_ref[u % 2, u // 2] < FIRST
-            order_ref[count] = u
-            return count + jnp.where(ready == (mode == "first"), 1, 0)
-        count = lax.fori_loop(0, 2 * n, sort, 0)
+        units = 2*UNIT
+        ready = idx_ref[units + 1, 0]
+        first_unit = 0 if mode == "first" else ready
+        count = ready if mode == "first" else 2*n - ready
 
     def place(i):
         if near:
             t = jnp.minimum(i, n - 1)
             return t, lambda k: idx_ref[k, t]
-        u = order_ref[jnp.maximum(jnp.minimum(i, count - 1), 0)]
-        t = u // 2
-        return t, lambda k: idx_ref[(u % 2) * UNIT + k, t]
+        u = idx_ref[units, first_unit + jnp.maximum(jnp.minimum(i, count - 1), 0)]
+        t = u & 31
+        half = lax.shift_right_logical(u, 5) * UNIT
+        return t, lambda k: idx_ref[half + k, t]
 
     def prep_w(t, slot):
         x = [jnp.broadcast_to(y_ref[c:c+1, lanes(t)] - cen_ref[t, c:c+1, :], (8, 128)) for c in range(3)]
@@ -221,11 +221,18 @@
 
     prep_all(0, 0)
 
-    def body(i, _):
-        for j in range(4):
-            step(4*i+j, j % 2)
-        return 0
-    lax.fori_loop(0, (count + 3)//4, body, 0)
+    def steps(many, start, stop):
+        def body(i, _):
+            for j in range(many):
+                step(start + many*i + j, j % 2)
+            return 0
+        lax.fori_loop(0, lax.div(stop - start + many - 1, many), body, 0)
+    if near:
+        steps(4, 0, count)
+    else:
+        most = count & ~7
+        steps(8, 0, most)
+        steps(2, most, count)
 
 
 VM = pl.BlockSpec(memory_space=pltpu.VMEM)
@@ -241,7 +248,7 @@
         scratch_shapes=[
             pltpu.VMEM((2, 128, 512), bf16), pltpu.VMEM((n, 8, 128), f32),
             pltpu.VMEM((n if mode == "near" else n_src, 48, 128), f32), pltpu.VMEM((24, 8, 128), f32),
-            pltpu.VMEM((2, n_src*128, 128), bf16), pltpu.SMEM((2*n+1,), jnp.int32)],
+            pltpu.VMEM((2, n_src*128, 128), bf16)],
         name=mode, cost_estimate=pl.CostEstimate(flops=COST[mode], bytes_accessed=1000000, transcendentals=0),
         compiler_params=pltpu.CompilerParams(vmem_limit_bytes=40 << 20),
     )(*scalars, *arrays)
@@ -250,7 +257,8 @@
 COST = {"near": 20000000000, "first": 16000000000, "rest": 6000000000}
 
 
-def request_kernel(owner_ref, slot_ref, want_ref, base_ref, top_ref):
+def request_kernel(owner_ref, slot_ref, y_ref, f_ref, want_ref, plan_ref, own_ref):
+    pack(y_ref, f_ref, own_ref)
     far, rows = owner_ref.shape
     groups = want_ref.shape[0]
     my_y, my_core = lax.axis_index("y"), lax.axis_index("core")
@@ -288,6 +296,8 @@
             if j != k:
                 p = p + jnp.where((mine[j] < mine[k]) if j > k else (mine[j] <= mine[k]), 1, 0)
         order.append(p)
+    plan_ref[...] = jnp.zeros(plan_ref.shape, jnp.int32)
+    tops = []
     for p in range(far):
         b = jnp.zeros((1, rows), jnp.int32)
         m = jnp.zeros((1, rows), jnp.int32)
@@ -295,12 +305,26 @@
             b = b + jnp.where(order[k] == p, base[k], 0)
             if p % UNIT == UNIT-1:
                 m = m + jnp.where(order[k] == p, mine[k], 0)
-        base_ref[p:p+1, :] = b
+        plan_ref[p:p+1, 0:rows] = b
         if p % UNIT == UNIT-1:
-            top_ref[p//UNIT:p//UNIT+1, :] = m
-
-
-def pack_kernel(y_ref, f_ref, after_ref, out_ref):
+            tops.append(m)
+    top = jnp.concatenate(tops + [jnp.full((1, 128 - 2*rows), CAP, jnp.int32)], 1)
+    unit = lax.broadcasted_iota(jnp.int32, (1, 128), 1)
+    ready = jnp.where((top < FIRST) & (unit < 2*rows), 1.0, 0.0)
+    lower = lax.broadcasted_iota(jnp.int32, (128, 128), 0) < lax.broadcasted_iota(jnp.int32, (128, 128), 1)
+    ahead = jnp.dot(jnp.broadcast_to(ready, (8, 128)).astype(bf16), lower.astype(f32).astype(bf16),
+                    preferred_element_type=f32)[0:1]
+    count = jnp.sum(ready, axis=1, keepdims=True)
+    spot = jnp.where(ready > 0.0, ahead, count + unit.astype(f32) - ahead)
+    spot = jnp.transpose(jnp.broadcast_to(spot, (128, 128)))
+    row = lax.broadcasted_iota(jnp.int32, (128, 128), 0)
+    lane = lax.broadcasted_iota(jnp.int32, (128, 128), 1).astype(f32)
+    listed = jnp.sum(jnp.where((spot == lane) & (row < 2*rows), row.astype(f32), 0.0), axis=0, keepdims=True)
+    plan_ref[far:far+1, :] = listed.astype(jnp.int32)
+    plan_ref[far+1:far+2, :] = jnp.broadcast_to(count, (1, 128)).astype(jnp.int32)
+
+
+def pack(y_ref, f_ref, out_ref):
     for t in range(y_ref.shape[1] // 128):
         out_ref[8*t:8*t+3, :] = y_ref[:, 128*t:128*t+128]
         out_ref[8*t+3:8*t+6, :] = f_ref[:, 128*t:128*t+128]
@@ -327,20 +351,17 @@
     far_count = far_owner.shape[1]
     groups = lax.axis_size("seg")
     i32 = jnp.int32
-    want, base, top = pl.pallas_call(
+    want, plan, own = pl.pallas_call(
         request_kernel,
-        out_shape=(jax.ShapeDtypeStruct((groups, 128), i32), jax.ShapeDtypeStruct((far_count, n), i32),
-                   jax.ShapeDtypeStruct((far_count//UNIT, n), i32)),
-        in_specs=[VM, VM], out_specs=(VM, VM, VM), name="requests",
-    )(far_owner.T, far_slot.T)
+        out_shape=(jax.ShapeDtypeStruct((groups, 128), i32), jax.ShapeDtypeStruct((far_count + 2, 128), i32),
+                   jax.ShapeDtypeStruct((8*n, 128), f32)),
+        in_specs=[VM]*4, out_specs=(VM, VM, VM), name="requests",
+    )(far_owner.T, far_slot.T, points, forces)
 
     def send(values):
         return lax.all_to_all(values, "seg", split_axis=0, concat_axis=0, tiled=True)
     asked = send(want.reshape(groups, 1, 128)).reshape(groups, 128)
 
-    own = pl.pallas_call(
-        pack_kernel, out_shape=jax.ShapeDtypeStruct((8*n, 128), f32), in_specs=[VM, VM, VM], out_specs=VM, name="pack",
-    )(points, forces, want)
     chip = jnp.concatenate([own, lax.ppermute(own, "core", [(0, 1), (1, 0)])], 0)
     tables = [chip] + [lax.ppermute(chip, "y", [(i, (i - d) % 4) for i in range(4)]) for d in (1, 2, 3)]
 
@@ -356,8 +377,8 @@
     reply_a, answers_a = answer(range(0, FIRST))
     near = pairs("near", near_count, (near_leaf.T, asked), (points, forces))
     reply_b, answers_b = answer(range(FIRST, CAP), near)
-    first = pairs("first", UNIT, (base, top), (points, near, answers_a))
-    return pairs("rest", UNIT, (base, top), (points, first, answers_a, answers_b))
+    first = pairs("first", UNIT, (plan,), (points, near, answers_a))
+    return pairs("rest", UNIT, (plan,), (points, first, answers_a, answers_b))
 
 
 def solution(mesh):

time: 87.4 us -> 83.5 us (0.955)
  Pallas kernels: 51.3 us -> 46.9 us
  other arithmetic: 0.92 us -> 0 us
  local copies, waits for them, and re-layouts: 0.02 us -> 0.94 us
    pallas_call x3, Pallas kernels: 43.1 us -> 39.8 us  [pairs(): pl.pallas_call(functools.partial(pair_kernel, mode, n_src), out_shape=jax...]
    pallas_call x1 -> x0, Pallas kernels: 1.55 us -> none  [per_device(): pl.pallas_call(pack_kernel, out_shape=jax.ShapeDtypeStruct((8 * n, 128),...]
    all_to_all x2, waiting for transfers between devices: 0.42 us -> 1.94 us  [send(): lax.all_to_all(values, 'seg', split_axis=0, concat_axis=0, tiled=True)]
    concatenate x1 -> x0, other arithmetic: 0.92 us -> none  [per_device(): jnp.concatenate([own, lax.ppermute(own, 'core', [(0, 1), (1, 0)])], 0)]
    ppermute x1, waiting for transfers between devices: 1.56 us -> 0.64 us  [per_device(): lax.ppermute(own, 'core', [(0, 1), (1, 0)])]
    unnamed x10 -> x9, local copies, waits for them, and re-layouts: 0.02 us -> 0.93 us
  transfers between devices with their start and end apart: 6 -> 6, of which waited for: 3 -> 3; matrix products, arithmetic and copies ran while one was open for 0% -> 1% of each run, Pallas kernels for 45% -> 45%
where the time goes in v3:
time: 83.5 us; the launch traced here: 82.7 us
  Pallas kernels  46.9 us (56%)
  starting transfers between devices  16.9 us (20%)
  blocking collectives  15.4 us (18%)
  waiting for transfers between devices  2.59 us (3%)
  local copies, waits for them, and re-layouts  0.94 us (1%)
    pallas_call x3, Pallas kernels, pairs(): pl.pallas_call(functools.partial(pair_kernel, mode, n_src), out_shape=jax...  39.8 us
    all_to_all x1, blocking collectives, send(): lax.all_to_all(values, 'seg', split_axis=0, concat_axis=0, tiled=True)  15.4 us
    all_to_all x2, starting transfers between devices, send(): lax.all_to_all(values, 'seg', split_axis=0, concat_axis=0, tiled=True)  10.9 us
    ppermute x3, starting transfers between devices, per_device(): lax.ppermute(chip, 'y', [(i, (i - d) % 4) for i in range(4)])  5.98 us
    pallas_call x2, Pallas kernels, answer(): pl.pallas_call(functools.partial(reply_kernel, ranks), out_shape=jax.Shap...  4.77 us
    pallas_call x1, Pallas kernels, per_device(): pl.pallas_call(request_kernel, out_shape=(jax.ShapeDtypeStruct((groups, 1...  2.31 us
    all_to_all x2, waiting for transfers between devices, send(): lax.all_to_all(values, 'seg', split_axis=0, concat_axis=0, tiled=True)  1.94 us
  transfers between devices with their start and end apart: 6, of which 3 were waited for; matrix products, arithmetic and copies ran while one was open for 1% of the time, Pallas kernels for 45%

profile of v3, /device:TPU:0, one launch (start us, length us, event | category | flops | bytes accessed | tf_op | source)
XLA Modules:
  0.0 82.7 jit_solution(4573836695354701852)
XLA Ops:
  0.0 2.3 %requests.1 = (s32[16,128]{1,0:T(8,128)}, s32[16,128]{1,0:T(8,128)}, f32[256,128]{1,0:T(8,128)}) custom-call(s32[14,32]{1,0:T(8,128)} %bitcast.16, s32[14,32]{1,0:T(8,128)} %bitcast.17, f32[3,4096]{1,0:T(4,128)} %refs_1_.3, f32[3,4096]{1,0:T(4,128)} %refs_3_.1), custom_call_target="tpu_custom_call" | custom-call | tf_op jit(solution)/shard_map/requests/pallas_call | solution.py:354
  2.3 0.0 collective-permute-start
  2.3 0.9 %constant_dynamic-update-slice_fusion.1 = f32[512,128]{1,0:T(8,128)S(1)} fusion(f32[256,128]{1,0:T(8,128)} %get-tuple-element.10), kind=kLoop, calls=%fused_computation.1 | loop fusion | bytes 262144
  3.2 0.6 collective-permute-done
  3.9 1.7 %collective-permute-start.3 = (f32[512,128]{1,0:T(8,128)S(1)}, f32[512,128]{1,0:T(8,128)S(1)}, u32[]{:S(2)}, u32[]{:S(2)}) collective-permute-start(f32[512,128]{1,0:T(8,128)S(1)} %constant_dynamic-update-slice_fusion.refs_1_), channel_id=1, source_target_pairs={{0,2},{2,4},{4,6},{6,0},{1,3},{3,5},{5,7},{7,1},{8,10},{10,12},{12... | collective-permute-start | bytes 786440 | tf_op jit(solution)/shard_map/ppermute | solution.py:366
  5.6 2.9 %collective-permute-start.2 = (f32[512,128]{1,0:T(8,128)S(1)}, f32[512,128]{1,0:T(8,128)S(1)}, u32[]{:S(2)}, u32[]{:S(2)}) collective-permute-start(f32[512,128]{1,0:T(8,128)S(1)} %constant_dynamic-update-slice_fusion.refs_1_), channel_id=1, source_target_pairs={{0,4},{2,6},{4,0},{6,2},{1,5},{3,7},{5,1},{7,3},{8,12},{10,14},{12... | collective-permute-start | bytes 786440 | tf_op jit(solution)/shard_map/ppermute | solution.py:366
  8.5 1.3 %collective-permute-start.1 = (f32[512,128]{1,0:T(8,128)S(1)}, f32[512,128]{1,0:T(8,128)S(1)}, u32[]{:S(2)}, u32[]{:S(2)}) collective-permute-start(f32[512,128]{1,0:T(8,128)S(1)} %constant_dynamic-update-slice_fusion.refs_1_), channel_id=1, source_target_pairs={{0,6},{2,0},{4,2},{6,4},{1,7},{3,1},{5,3},{7,5},{8,14},{10,8},{12,... | collective-permute-start | bytes 786440 | tf_op jit(solution)/shard_map/ppermute | solution.py:366
  9.9 15.4 %all_to_all.15 = s32[16,1,128]{2,1,0:T(1,128)S(1)} all-to-all(s32[16,1,128]{2,1,0:T(1,128)} %bitcast.18), channel_id=1, replica_groups=mesh['seg'=16,'y'=4,'core'=2] {'seg'}, dimensions={0} | all-to-all | bytes 16384 | tf_op jit(solution)/shard_map/all_to_all | solution.py:362
  25.2 0.0 collective-permute-done.3.refs_4_
  25.2 0.0 collective-permute-done.2.refs_3_
  25.2 0.0 collective-permute-done.1.refs_2_
  25.2 2.4 %replies.2 = f32[16,168,128]{2,1,0:T(8,128)} custom-call(s32[16,128]{1,0:T(8,128)S(1)} %bitcast.12, f32[512,128]{1,0:T(8,128)S(1)} %constant_dynamic-update-slice_fusion.refs_1_, f32[512,128]{1,0:T(8,128)S(1)} %collective-permute-done.1.refs_2_, f32[512,128]{1,0:T(8,128)S(1)} %collective-permute-done.2.refs_3_, f32[512,128]{1,0:T(8,128)S(1)} %collective-permute-done.3.refs_4_), custom_call_target="tpu_custom_call" | custom-call | tf_op jit(solution)/shard_map/replies/pallas_call | solution.py:369
  27.6 3.8 %all-to-all-start.1 = ((f32[16,168,128]{2,1,0:T(8,128)}), f32[16,168,128]{2,1,0:T(8,128)S(1)}, u32[]{:S(2)}, u32[]{:S(2)}) async-start(f32[16,168,128]{2,1,0:T(8,128)} %replies.2), calls=%async_computation.1 | async-start | bytes 2752512 | tf_op jit(solution)/shard_map/all_to_all | solution.py:362
  31.5 0.0 copy-done
  31.5 0.0 copy-done.1
  31.5 0.0 copy-done.2
  31.5 17.5 %near.1.refs_2_.refs_5_ = f32[3,4096]{1,0:T(4,128)S(1)} custom-call(s32[13,32]{1,0:T(8,128)S(1)} %bitcast.15, s32[16,128]{1,0:T(8,128)S(1)} %bitcast.13, f32[3,4096]{1,0:T(4,128)S(1)} %copy-done.1, f32[3,4096]{1,0:T(4,128)S(1)} %copy-done), custom_call_target="tpu_custom_call" | custom-call | flops 20000000000 | bytes 1000000 | tf_op jit(solution)/shard_map/near/pallas_call | solution.py:244
  49.0 2.4 %replies.3 = f32[16,168,128]{2,1,0:T(8,128)} custom-call(s32[16,128]{1,0:T(8,128)S(1)} %bitcast.14, f32[512,128]{1,0:T(8,128)S(1)} %constant_dynamic-update-slice_fusion.refs_1_, f32[512,128]{1,0:T(8,128)S(1)} %collective-permute-done.1.refs_2_, f32[512,128]{1,0:T(8,128)S(1)} %collective-permute-done.2.refs_3_, ...), custom_call_target="tpu_custom_call" | custom-call | tf_op jit(solution)/shard_map/replies/pallas_call | solution.py:369
  51.4 0.2 all-to-all-done.1
  51.6 7.1 %all-to-all-start.2 = ((f32[16,168,128]{2,1,0:T(8,128)}), f32[16,168,128]{2,1,0:T(8,128)S(1)}, u32[]{:S(2)}, u32[]{:S(2)}) async-start(f32[16,168,128]{2,1,0:T(8,128)} %replies.3), calls=%async_computation.2 | async-start | bytes 2752512 | tf_op jit(solution)/shard_map/all_to_all | solution.py:362
  58.7 0.0 copy-done.3
  58.7 17.6 %first.1.refs_2_ = f32[3,4096]{1,0:T(4,128)S(1)} custom-call(s32[16,128]{1,0:T(8,128)S(1)} %copy-done.3, f32[3,4096]{1,0:T(4,128)S(1)} %copy-done.1, f32[3,4096]{1,0:T(4,128)S(1)} %near.1.refs_2_.refs_5_, f32[2688,128]{1,0:T(8,128)S(1)} %bitcast.9), custom_call_target="tpu_custom_call" | custom-call | flops 16000000000 | bytes 1000000 | tf_op jit(solution)/shard_map/first/pallas_call | solution.py:244
  76.3 1.7 %all-to-all-done.2 = f32[16,168,128]{2,1,0:T(8,128)S(1)} async-done(((f32[16,168,128]{2,1,0:T(8,128)}), f32[16,168,128]{2,1,0:T(8,128)S(1)}, u32[]{:S(2)}, u32[]{:S(2)}) %all-to-all-start.2) | async-done | bytes 1376288 | tf_op jit(solution)/shard_map/all_to_all | solution.py:362
  78.0 4.7 %rest.1 = f32[3,4096]{1,0:T(4,128)} custom-call(s32[16,128]{1,0:T(8,128)S(1)} %copy-done.3, f32[3,4096]{1,0:T(4,128)S(1)} %copy-done.1, f32[3,4096]{1,0:T(4,128)S(1)} %first.1.refs_2_, f32[2688,128]{1,0:T(8,128)S(1)} %bitcast.10, f32[2688,128]{1,0:T(8,128)S(1)} %bitcast.11), custom_call_target="tpu_custom_call" | custom-call | flops 6000000000 | bytes 1000000 | tf_op jit(solution)/shard_map/rest/pallas_call | solution.py:244
  (5 shorter events, 0.0 us)
Async XLA Ops:
  2.3 1.6 %collective-permute-start = (f32[256,128]{1,0:T(8,128)}, f32[256,128]{1,0:T(8,128)S(1)}, u32[]{:S(2)}, u32[]{:S(2)}) collective-permute-start(f32[256,128]{1,0:T(8,128)} %get-tuple-element.10), channel_id=1, source_target_pairs={{0,1},{1,0},{2,3},{3,2},{4,5},{5,4},{6,7},{7,6},{8,9},{9,8},{10,11... | collective-permute-start | bytes 393224 | tf_op jit(solution)/shard_map/ppermute | solution.py:365
  3.9 21.3 %collective-permute-start.3 = (f32[512,128]{1,0:T(8,128)S(1)}, f32[512,128]{1,0:T(8,128)S(1)}, u32[]{:S(2)}, u32[]{:S(2)}) collective-permute-start(f32[512,128]{1,0:T(8,128)S(1)} %constant_dynamic-update-slice_fusion.refs_1_), channel_id=1, source_target_pairs={{0,2},{2,4},{4,6},{6,0},{1,3},{3,5},{5,7},{7,1},{8,10},{10,12},{12... | collective-permute-start | bytes 786440 | tf_op jit(solution)/shard_map/ppermute | solution.py:366
  5.6 19.6 %collective-permute-start.2 = (f32[512,128]{1,0:T(8,128)S(1)}, f32[512,128]{1,0:T(8,128)S(1)}, u32[]{:S(2)}, u32[]{:S(2)}) collective-permute-start(f32[512,128]{1,0:T(8,128)S(1)} %constant_dynamic-update-slice_fusion.refs_1_), channel_id=1, source_target_pairs={{0,4},{2,6},{4,0},{6,2},{1,5},{3,7},{5,1},{7,3},{8,12},{10,14},{12... | collective-permute-start | bytes 786440 | tf_op jit(solution)/shard_map/ppermute | solution.py:366
  8.5 16.7 %collective-permute-start.1 = (f32[512,128]{1,0:T(8,128)S(1)}, f32[512,128]{1,0:T(8,128)S(1)}, u32[]{:S(2)}, u32[]{:S(2)}) collective-permute-start(f32[512,128]{1,0:T(8,128)S(1)} %constant_dynamic-update-slice_fusion.refs_1_), channel_id=1, source_target_pairs={{0,6},{2,0},{4,2},{6,4},{1,7},{3,1},{5,3},{7,5},{8,14},{10,8},{12,... | collective-permute-start | bytes 786440 | tf_op jit(solution)/shard_map/ppermute | solution.py:366
  27.6 3.9 %copy-start = (f32[3,4096]{1,0:T(4,128)S(1)}, f32[3,4096]{1,0:T(4,128)}, u32[]{:S(2)}) copy-start(f32[3,4096]{1,0:T(4,128)} %refs_3_.1) | copy-start | bytes 147460
  27.6 3.9 %copy-start.1 = (f32[3,4096]{1,0:T(4,128)S(1)}, f32[3,4096]{1,0:T(4,128)}, u32[]{:S(2)}) copy-start(f32[3,4096]{1,0:T(4,128)} %refs_1_.3) | copy-start | bytes 147460
  27.6 3.9 %copy-start.2 = (s32[32,13]{0,1:T(8,128)S(1)}, s32[32,13]{0,1:T(8,128)}, u32[]{:S(2)}) copy-start(s32[32,13]{0,1:T(8,128)} %param.7) | copy-start | bytes 4996
  27.6 24.0 %all-to-all-start.1 = ((f32[16,168,128]{2,1,0:T(8,128)}), f32[16,168,128]{2,1,0:T(8,128)S(1)}, u32[]{:S(2)}, u32[]{:S(2)}) async-start(f32[16,168,128]{2,1,0:T(8,128)} %replies.2), calls=%async_computation.1 | async-start | bytes 2752512 | tf_op jit(solution)/shard_map/all_to_all | solution.py:362
  51.4 7.3 %copy-start.3 = (s32[16,128]{1,0:T(8,128)S(1)}, s32[16,128]{1,0:T(8,128)}, u32[]{:S(2)}) copy-start(s32[16,128]{1,0:T(8,128)} %get-tuple-element.8.refs_0_) | copy-start | bytes 24580
  51.6 26.4 %all-to-all-start.2 = ((f32[16,168,128]{2,1,0:T(8,128)}), f32[16,168,128]{2,1,0:T(8,128)S(1)}, u32[]{:S(2)}, u32[]{:S(2)}) async-start(f32[16,168,128]{2,1,0:T(8,128)} %replies.3), calls=%async_computation.2 | async-start | bytes 2752512 | tf_op jit(solution)/shard_map/all_to_all | solution.py:362

commit v4 on v3

--- a/solution.py
+++ b/solution.py
@@ -18,9 +18,9 @@
 QK = B / C1 * K2
 KE = K2 * E * E
 CAP = 56
-FIRST = 28
-PER_A = 6 * FIRST
-PER_B = 6 * (CAP - FIRST)
+FIRST = 30
+PER_A = 184
+PER_B = 160
 UNIT = 7
 f32 = jnp.float32
 bf16 = jnp.bfloat16
@@ -228,7 +228,7 @@
             return 0
         lax.fori_loop(0, lax.div(stop - start + many - 1, many), body, 0)
     if near:
-        steps(4, 0, count)
+        steps(8, 0, count)
     else:
         most = count & ~7
         steps(8, 0, most)
@@ -326,17 +326,18 @@
 
 def pack(y_ref, f_ref, out_ref):
     for t in range(y_ref.shape[1] // 128):
-        out_ref[8*t:8*t+3, :] = y_ref[:, 128*t:128*t+128]
-        out_ref[8*t+3:8*t+6, :] = f_ref[:, 128*t:128*t+128]
-        out_ref[8*t+6:8*t+8, :] = jnp.zeros((2, 128), f32)
+        out_ref[6*t:6*t+3, :] = y_ref[:, 128*t:128*t+128]
+        out_ref[6*t+3:6*t+6, :] = f_ref[:, 128*t:128*t+128]
 
 
 def reply_kernel(ranks, *refs):
     ask_ref, *tables = refs[:5]
     out_ref, table_ref = refs[-2:]
-    rows = tables[0].shape[0]
+    leaves = tables[0].shape[0] // 6
     for i, ref in enumerate(tables):
-        table_ref[rows*i:rows*i+rows, :] = ref[...]
+        for k in range(leaves):
+            to = 8*(leaves*i + k)
+            table_ref[to:to+6, :] = ref[6*k:6*k+6, :]
 
     def one(p, _):
         for q, r in enumerate(ranks):
@@ -354,7 +355,7 @@
     want, plan, own = pl.pallas_call(
         request_kernel,
         out_shape=(jax.ShapeDtypeStruct((groups, 128), i32), jax.ShapeDtypeStruct((far_count + 2, 128), i32),
-                   jax.ShapeDtypeStruct((8*n, 128), f32)),
+                   jax.ShapeDtypeStruct((6*n, 128), f32)),
         in_specs=[VM]*4, out_specs=(VM, VM, VM), name="requests",
     )(far_owner.T, far_slot.T, points, forces)
 
@@ -365,18 +366,18 @@
     chip = jnp.concatenate([own, lax.ppermute(own, "core", [(0, 1), (1, 0)])], 0)
     tables = [chip] + [lax.ppermute(chip, "y", [(i, (i - d) % 4) for i in range(4)]) for d in (1, 2, 3)]
 
-    def answer(ranks, *after):
+    def answer(per, ranks, *after):
         reply = pl.pallas_call(
             functools.partial(reply_kernel, ranks),
-            out_shape=jax.ShapeDtypeStruct((groups, 6*len(ranks), 128), f32),
+            out_shape=jax.ShapeDtypeStruct((groups, per, 128), f32),
             in_specs=[SM] + [VM]*(4 + len(after)), out_specs=VM,
             scratch_shapes=[pltpu.VMEM((64*n, 128), f32)], name="replies",
             compiler_params=pltpu.CompilerParams(vmem_limit_bytes=32 << 20),
         )(asked, *tables, *after)
         return reply, send(reply).reshape(-1, 128)
-    reply_a, answers_a = answer(range(0, FIRST))
+    reply_a, answers_a = answer(PER_A, range(0, FIRST))
     near = pairs("near", near_count, (near_leaf.T, asked), (points, forces))
-    reply_b, answers_b = answer(range(FIRST, CAP), near)
+    reply_b, answers_b = answer(PER_B, range(FIRST, CAP), near)
     first = pairs("first", UNIT, (plan,), (points, near, answers_a))
     return pairs("rest", UNIT, (plan,), (points, first, answers_a, answers_b))
 

time: 83.5 us -> 80.2 us (0.960)
  starting transfers between devices: 16.9 us -> 12.3 us
  waiting for transfers between devices: 2.59 us -> 4.81 us
    all_to_all x2, starting transfers between devices: 10.9 us -> 7.54 us  [send(): lax.all_to_all(values, 'seg', split_axis=0, concat_axis=0, tiled=True)]
    all_to_all x2, waiting for transfers between devices: 1.94 us -> 4.19 us  [send(): lax.all_to_all(values, 'seg', split_axis=0, concat_axis=0, tiled=True)]
    ppermute x3, starting transfers between devices: 5.98 us -> 4.77 us  [per_device(): lax.ppermute(chip, 'y', [(i, (i - d) % 4) for i in range(4)])]
  transfers between devices with their start and end apart: 6 -> 6, of which waited for: 3 -> 3; matrix products, arithmetic and copies ran while one was open for 1% -> 1% of each run, Pallas kernels for 45% -> 48%
where the time goes in v4:
time: 80.2 us; the launch traced here: 79.8 us
  Pallas kernels  46.3 us (58%)
  blocking collectives  15.4 us (19%)
  starting transfers between devices  12.3 us (15%)
  waiting for transfers between devices  4.81 us (6%)
  local copies, waits for them, and re-layouts  0.92 us (1%)
    pallas_call x3, Pallas kernels, pairs(): pl.pallas_call(functools.partial(pair_kernel, mode, n_src), out_shape=jax...  39.2 us
    all_to_all x1, blocking collectives, send(): lax.all_to_all(values, 'seg', split_axis=0, concat_axis=0, tiled=True)  15.4 us
    all_to_all x2, starting transfers between devices, send(): lax.all_to_all(values, 'seg', split_axis=0, concat_axis=0, tiled=True)  7.54 us
    pallas_call x2, Pallas kernels, answer(): pl.pallas_call(functools.partial(reply_kernel, ranks), out_shape=jax.Shap...  4.83 us
    ppermute x3, starting transfers between devices, per_device(): lax.ppermute(chip, 'y', [(i, (i - d) % 4) for i in range(4)])  4.77 us
    all_to_all x2, waiting for transfers between devices, send(): lax.all_to_all(values, 'seg', split_axis=0, concat_axis=0, tiled=True)  4.19 us
    pallas_call x1, Pallas kernels, per_device(): pl.pallas_call(request_kernel, out_shape=(jax.ShapeDtypeStruct((groups, 1...  2.29 us
  transfers between devices with their start and end apart: 6, of which 3 were waited for; matrix products, arithmetic and copies ran while one was open for 1% of the time, Pallas kernels for 48%

profile of v4, /device:TPU:0, one launch (start us, length us, event | category | flops | bytes accessed | tf_op | source)
XLA Modules:
  0.0 79.8 jit_solution(15139677750440699835)
XLA Ops:
  0.0 2.3 %requests.1 = (s32[16,128]{1,0:T(8,128)}, s32[16,128]{1,0:T(8,128)}, f32[192,128]{1,0:T(8,128)}) custom-call(s32[14,32]{1,0:T(8,128)} %bitcast.16, s32[14,32]{1,0:T(8,128)} %bitcast.17, f32[3,4096]{1,0:T(4,128)} %refs_1_.3, f32[3,4096]{1,0:T(4,128)} %refs_3_.1), custom_call_target="tpu_custom_call" | custom-call | tf_op jit(solution)/shard_map/requests/pallas_call | solution.py:355
  2.3 0.0 collective-permute-start
  2.3 0.9 %constant_dynamic-update-slice_fusion.1 = f32[384,128]{1,0:T(8,128)S(1)} fusion(f32[192,128]{1,0:T(8,128)} %get-tuple-element.10), kind=kLoop, calls=%fused_computation.1 | loop fusion | bytes 196608
  3.2 0.6 collective-permute-done
  3.8 3.2 %collective-permute-start.1 = (f32[384,128]{1,0:T(8,128)S(1)}, f32[384,128]{1,0:T(8,128)S(1)}, u32[]{:S(2)}, u32[]{:S(2)}) collective-permute-start(f32[384,128]{1,0:T(8,128)S(1)} %constant_dynamic-update-slice_fusion.refs_1_), channel_id=1, source_target_pairs={{0,6},{2,0},{4,2},{6,4},{1,7},{3,1},{5,3},{7,5},{8,14},{10,8},{12,... | collective-permute-start | bytes 589832 | tf_op jit(solution)/shard_map/ppermute | solution.py:367
  7.0 0.6 collective-permute-start.2
  7.6 1.0 %collective-permute-start.3 = (f32[384,128]{1,0:T(8,128)S(1)}, f32[384,128]{1,0:T(8,128)S(1)}, u32[]{:S(2)}, u32[]{:S(2)}) collective-permute-start(f32[384,128]{1,0:T(8,128)S(1)} %constant_dynamic-update-slice_fusion.refs_1_), channel_id=1, source_target_pairs={{0,2},{2,4},{4,6},{6,0},{1,3},{3,5},{5,7},{7,1},{8,10},{10,12},{12... | collective-permute-start | bytes 589832 | tf_op jit(solution)/shard_map/ppermute | solution.py:367
  8.6 15.4 %all_to_all.15 = s32[16,1,128]{2,1,0:T(1,128)S(1)} all-to-all(s32[16,1,128]{2,1,0:T(1,128)} %bitcast.18), channel_id=1, replica_groups=mesh['seg'=16,'y'=4,'core'=2] {'seg'}, dimensions={0} | all-to-all | bytes 16384 | tf_op jit(solution)/shard_map/all_to_all | solution.py:363
  23.9 0.0 collective-permute-done.1.refs_2_
  23.9 0.0 collective-permute-done.2.refs_3_
  24.0 0.0 collective-permute-done.3.refs_4_
  24.0 2.5 %replies.2 = f32[16,184,128]{2,1,0:T(8,128)} custom-call(s32[16,128]{1,0:T(8,128)S(1)} %bitcast.12, f32[384,128]{1,0:T(8,128)S(1)} %constant_dynamic-update-slice_fusion.refs_1_, f32[384,128]{1,0:T(8,128)S(1)} %collective-permute-done.1.refs_2_, f32[384,128]{1,0:T(8,128)S(1)} %collective-permute-done.2.refs_3_, f32[384,128]{1,0:T(8,128)S(1)} %collective-permute-done.3.refs_4_), custom_call_target="tpu_custom_call" | custom-call | tf_op jit(solution)/shard_map/replies/pallas_call | solution.py:370
  26.4 3.8 %all-to-all-start.1 = ((f32[16,184,128]{2,1,0:T(8,128)}), f32[16,184,128]{2,1,0:T(8,128)S(1)}, u32[]{:S(2)}, u32[]{:S(2)}) async-start(f32[16,184,128]{2,1,0:T(8,128)} %replies.2), calls=%async_computation.1 | async-start | bytes 3014656 | tf_op jit(solution)/shard_map/all_to_all | solution.py:363
  30.3 0.0 copy-done
  30.3 0.0 copy-done.1
  30.3 0.0 copy-done.2
  30.3 16.7 %near.1.refs_2_.refs_5_ = f32[3,4096]{1,0:T(4,128)S(1)} custom-call(s32[13,32]{1,0:T(8,128)S(1)} %bitcast.15, s32[16,128]{1,0:T(8,128)S(1)} %bitcast.13, f32[3,4096]{1,0:T(4,128)S(1)} %copy-done.1, f32[3,4096]{1,0:T(4,128)S(1)} %copy-done), custom_call_target="tpu_custom_call" | custom-call | flops 20000000000 | bytes 1000000 | tf_op jit(solution)/shard_map/near/pallas_call | solution.py:244
  47.0 2.4 %replies.3 = f32[16,160,128]{2,1,0:T(8,128)} custom-call(s32[16,128]{1,0:T(8,128)S(1)} %bitcast.14, f32[384,128]{1,0:T(8,128)S(1)} %constant_dynamic-update-slice_fusion.refs_1_, f32[384,128]{1,0:T(8,128)S(1)} %collective-permute-done.1.refs_2_, f32[384,128]{1,0:T(8,128)S(1)} %collective-permute-done.2.refs_3_, ...), custom_call_target="tpu_custom_call" | custom-call | tf_op jit(solution)/shard_map/replies/pallas_call | solution.py:370
  49.4 3.7 %all-to-all-done.1 = f32[16,184,128]{2,1,0:T(8,128)S(1)} async-done(((f32[16,184,128]{2,1,0:T(8,128)}), f32[16,184,128]{2,1,0:T(8,128)S(1)}, u32[]{:S(2)}, u32[]{:S(2)}) %all-to-all-start.1) | async-done | bytes 1507360 | tf_op jit(solution)/shard_map/all_to_all | solution.py:363
  53.1 3.7 %all-to-all-start.2 = ((f32[16,160,128]{2,1,0:T(8,128)}), f32[16,160,128]{2,1,0:T(8,128)S(1)}, u32[]{:S(2)}, u32[]{:S(2)}) async-start(f32[16,160,128]{2,1,0:T(8,128)} %replies.3), calls=%async_computation.2 | async-start | bytes 2621440 | tf_op jit(solution)/shard_map/all_to_all | solution.py:363
  56.8 0.0 copy-done.3
  56.8 19.2 %first.1.refs_2_ = f32[3,4096]{1,0:T(4,128)S(1)} custom-call(s32[16,128]{1,0:T(8,128)S(1)} %copy-done.3, f32[3,4096]{1,0:T(4,128)S(1)} %copy-done.1, f32[3,4096]{1,0:T(4,128)S(1)} %near.1.refs_2_.refs_5_, f32[2944,128]{1,0:T(8,128)S(1)} %bitcast.9), custom_call_target="tpu_custom_call" | custom-call | flops 16000000000 | bytes 1000000 | tf_op jit(solution)/shard_map/first/pallas_call | solution.py:244
  76.0 0.5 all-to-all-done.2
  76.5 3.2 %rest.1 = f32[3,4096]{1,0:T(4,128)} custom-call(s32[16,128]{1,0:T(8,128)S(1)} %copy-done.3, f32[3,4096]{1,0:T(4,128)S(1)} %copy-done.1, f32[3,4096]{1,0:T(4,128)S(1)} %first.1.refs_2_, f32[2944,128]{1,0:T(8,128)S(1)} %bitcast.10, f32[2560,128]{1,0:T(8,128)S(1)} %bitcast.11), custom_call_target="tpu_custom_call" | custom-call | flops 6000000000 | bytes 1000000 | tf_op jit(solution)/shard_map/rest/pallas_call | solution.py:244
  (5 shorter events, 0.0 us)
Async XLA Ops:
  2.3 1.5 %collective-permute-start = (f32[192,128]{1,0:T(8,128)}, f32[192,128]{1,0:T(8,128)S(1)}, u32[]{:S(2)}, u32[]{:S(2)}) collective-permute-start(f32[192,128]{1,0:T(8,128)} %get-tuple-element.10), channel_id=1, source_target_pairs={{0,1},{1,0},{2,3},{3,2},{4,5},{5,4},{6,7},{7,6},{8,9},{9,8},{10,11... | collective-permute-start | bytes 294920 | tf_op jit(solution)/shard_map/ppermute | solution.py:366
  3.8 20.1 %collective-permute-start.1 = (f32[384,128]{1,0:T(8,128)S(1)}, f32[384,128]{1,0:T(8,128)S(1)}, u32[]{:S(2)}, u32[]{:S(2)}) collective-permute-start(f32[384,128]{1,0:T(8,128)S(1)} %constant_dynamic-update-slice_fusion.refs_1_), channel_id=1, source_target_pairs={{0,6},{2,0},{4,2},{6,4},{1,7},{3,1},{5,3},{7,5},{8,14},{10,8},{12,... | collective-permute-start | bytes 589832 | tf_op jit(solution)/shard_map/ppermute | solution.py:367
  7.0 17.0 %collective-permute-start.2 = (f32[384,128]{1,0:T(8,128)S(1)}, f32[384,128]{1,0:T(8,128)S(1)}, u32[]{:S(2)}, u32[]{:S(2)}) collective-permute-start(f32[384,128]{1,0:T(8,128)S(1)} %constant_dynamic-update-slice_fusion.refs_1_), channel_id=1, source_target_pairs={{0,4},{2,6},{4,0},{6,2},{1,5},{3,7},{5,1},{7,3},{8,12},{10,14},{12... | collective-permute-start | bytes 589832 | tf_op jit(solution)/shard_map/ppermute | solution.py:367
  7.6 16.3 %collective-permute-start.3 = (f32[384,128]{1,0:T(8,128)S(1)}, f32[384,128]{1,0:T(8,128)S(1)}, u32[]{:S(2)}, u32[]{:S(2)}) collective-permute-start(f32[384,128]{1,0:T(8,128)S(1)} %constant_dynamic-update-slice_fusion.refs_1_), channel_id=1, source_target_pairs={{0,2},{2,4},{4,6},{6,0},{1,3},{3,5},{5,7},{7,1},{8,10},{10,12},{12... | collective-permute-start | bytes 589832 | tf_op jit(solution)/shard_map/ppermute | solution.py:367
  26.4 3.9 %copy-start = (f32[3,4096]{1,0:T(4,128)S(1)}, f32[3,4096]{1,0:T(4,128)}, u32[]{:S(2)}) copy-start(f32[3,4096]{1,0:T(4,128)} %refs_3_.1) | copy-start | bytes 147460
  26.4 3.9 %copy-start.1 = (f32[3,4096]{1,0:T(4,128)S(1)}, f32[3,4096]{1,0:T(4,128)}, u32[]{:S(2)}) copy-start(f32[3,4096]{1,0:T(4,128)} %refs_1_.3) | copy-start | bytes 147460
  26.4 3.9 %copy-start.2 = (s32[32,13]{0,1:T(8,128)S(1)}, s32[32,13]{0,1:T(8,128)}, u32[]{:S(2)}) copy-start(s32[32,13]{0,1:T(8,128)} %param.7) | copy-start | bytes 4996
  26.4 26.6 %all-to-all-start.1 = ((f32[16,184,128]{2,1,0:T(8,128)}), f32[16,184,128]{2,1,0:T(8,128)S(1)}, u32[]{:S(2)}, u32[]{:S(2)}) async-start(f32[16,184,128]{2,1,0:T(8,128)} %replies.2), calls=%async_computation.1 | async-start | bytes 3014656 | tf_op jit(solution)/shard_map/all_to_all | solution.py:363
  49.4 7.4 %copy-start.3 = (s32[16,128]{1,0:T(8,128)S(1)}, s32[16,128]{1,0:T(8,128)}, u32[]{:S(2)}) copy-start(s32[16,128]{1,0:T(8,128)} %get-tuple-element.8.refs_0_) | copy-start | bytes 24580
  53.1 23.4 %all-to-all-start.2 = ((f32[16,160,128]{2,1,0:T(8,128)}), f32[16,160,128]{2,1,0:T(8,128)S(1)}, u32[]{:S(2)}, u32[]{:S(2)}) async-start(f32[16,160,128]{2,1,0:T(8,128)} %replies.3), calls=%async_computation.2 | async-start | bytes 2621440 | tf_op jit(solution)/shard_map/all_to_all | solution.py:363

commit v5 on v4

--- a/solution.py
+++ b/solution.py
@@ -18,9 +18,9 @@
 QK = B / C1 * K2
 KE = K2 * E * E
 CAP = 56
-FIRST = 30
-PER_A = 184
-PER_B = 160
+FIRST = 32
+PER_A = 192
+PER_B = 144
 UNIT = 7
 f32 = jnp.float32
 bf16 = jnp.bfloat16

time: 80.2 us -> 80.6 us (level)
  transfers between devices with their start and end apart: 6 -> 6, of which waited for: 3 -> 2; matrix products, arithmetic and copies ran while one was open for 1% -> 1% of each run, Pallas kernels for 48% -> 46%
where the time goes in v5:
time: 80.6 us; the launch traced here: 79.5 us
  Pallas kernels  45.6 us (57%)
  blocking collectives  15.4 us (19%)
  starting transfers between devices  12.3 us (15%)
  waiting for transfers between devices  5.16 us (6%)
  local copies, waits for them, and re-layouts  0.92 us (1%)
    pallas_call x3, Pallas kernels, pairs(): pl.pallas_call(functools.partial(pair_kernel, mode, n_src), out_shape=jax...  38.5 us
    all_to_all x1, blocking collectives, send(): lax.all_to_all(values, 'seg', split_axis=0, concat_axis=0, tiled=True)  15.4 us
    all_to_all x2, starting transfers between devices, send(): lax.all_to_all(values, 'seg', split_axis=0, concat_axis=0, tiled=True)  7.54 us
    pallas_call x2, Pallas kernels, answer(): pl.pallas_call(functools.partial(reply_kernel, ranks), out_shape=jax.Shap...  4.8 us
    ppermute x3, starting transfers between devices, per_device(): lax.ppermute(chip, 'y', [(i, (i - d) % 4) for i in range(4)])  4.77 us
    all_to_all x2, waiting for transfers between devices, send(): lax.all_to_all(values, 'seg', split_axis=0, concat_axis=0, tiled=True)  4.54 us
    pallas_call x1, Pallas kernels, per_device(): pl.pallas_call(request_kernel, out_shape=(jax.ShapeDtypeStruct((groups, 1...  2.29 us
  transfers between devices with their start and end apart: 6, of which 2 were waited for; matrix products, arithmetic and copies ran while one was open for 1% of the time, Pallas kernels for 46%

profile of v5, /device:TPU:0, one launch (start us, length us, event | category | flops | bytes accessed | tf_op | source)
XLA Modules:
  0.0 79.5 jit_solution(17157361155117789751)
XLA Ops:
  0.0 2.3 %requests.1 = (s32[16,128]{1,0:T(8,128)}, s32[16,128]{1,0:T(8,128)}, f32[192,128]{1,0:T(8,128)}) custom-call(s32[14,32]{1,0:T(8,128)} %bitcast.16, s32[14,32]{1,0:T(8,128)} %bitcast.17, f32[3,4096]{1,0:T(4,128)} %refs_1_.3, f32[3,4096]{1,0:T(4,128)} %refs_3_.1), custom_call_target="tpu_custom_call" | custom-call | tf_op jit(solution)/shard_map/requests/pallas_call | solution.py:355
  2.3 0.0 collective-permute-start
  2.3 0.9 %constant_dynamic-update-slice_fusion.1 = f32[384,128]{1,0:T(8,128)S(1)} fusion(f32[192,128]{1,0:T(8,128)} %get-tuple-element.10), kind=kLoop, calls=%fused_computation.1 | loop fusion | bytes 196608
  3.2 0.6 collective-permute-done
  3.8 3.2 %collective-permute-start.1 = (f32[384,128]{1,0:T(8,128)S(1)}, f32[384,128]{1,0:T(8,128)S(1)}, u32[]{:S(2)}, u32[]{:S(2)}) collective-permute-start(f32[384,128]{1,0:T(8,128)S(1)} %constant_dynamic-update-slice_fusion.refs_1_), channel_id=1, source_target_pairs={{0,6},{2,0},{4,2},{6,4},{1,7},{3,1},{5,3},{7,5},{8,14},{10,8},{12,... | collective-permute-start | bytes 589832 | tf_op jit(solution)/shard_map/ppermute | solution.py:367
  7.0 0.6 collective-permute-start.2
  7.6 1.0 %collective-permute-start.3 = (f32[384,128]{1,0:T(8,128)S(1)}, f32[384,128]{1,0:T(8,128)S(1)}, u32[]{:S(2)}, u32[]{:S(2)}) collective-permute-start(f32[384,128]{1,0:T(8,128)S(1)} %constant_dynamic-update-slice_fusion.refs_1_), channel_id=1, source_target_pairs={{0,2},{2,4},{4,6},{6,0},{1,3},{3,5},{5,7},{7,1},{8,10},{10,12},{12... | collective-permute-start | bytes 589832 | tf_op jit(solution)/shard_map/ppermute | solution.py:367
  8.6 15.4 %all_to_all.15 = s32[16,1,128]{2,1,0:T(1,128)S(1)} all-to-all(s32[16,1,128]{2,1,0:T(1,128)} %bitcast.18), channel_id=1, replica_groups=mesh['seg'=16,'y'=4,'core'=2] {'seg'}, dimensions={0} | all-to-all | bytes 16384 | tf_op jit(solution)/shard_map/all_to_all | solution.py:363
  23.9 0.0 collective-permute-done.1.refs_2_
  23.9 0.0 collective-permute-done.2.refs_3_
  24.0 0.0 collective-permute-done.3.refs_4_
  24.0 2.5 %replies.2 = f32[16,192,128]{2,1,0:T(8,128)} custom-call(s32[16,128]{1,0:T(8,128)S(1)} %bitcast.12, f32[384,128]{1,0:T(8,128)S(1)} %constant_dynamic-update-slice_fusion.refs_1_, f32[384,128]{1,0:T(8,128)S(1)} %collective-permute-done.1.refs_2_, f32[384,128]{1,0:T(8,128)S(1)} %collective-permute-done.2.refs_3_, f32[384,128]{1,0:T(8,128)S(1)} %collective-permute-done.3.refs_4_), custom_call_target="tpu_custom_call" | custom-call | tf_op jit(solution)/shard_map/replies/pallas_call | solution.py:370
  26.5 3.8 %all-to-all-start.1 = ((f32[16,192,128]{2,1,0:T(8,128)}), f32[16,192,128]{2,1,0:T(8,128)S(1)}, u32[]{:S(2)}, u32[]{:S(2)}) async-start(f32[16,192,128]{2,1,0:T(8,128)} %replies.2), calls=%async_computation.1 | async-start | bytes 3145728 | tf_op jit(solution)/shard_map/all_to_all | solution.py:363
  30.4 0.0 copy-done
  30.4 0.0 copy-done.1
  30.4 0.0 copy-done.2
  30.4 16.7 %near.1.refs_2_.refs_5_ = f32[3,4096]{1,0:T(4,128)S(1)} custom-call(s32[13,32]{1,0:T(8,128)S(1)} %bitcast.15, s32[16,128]{1,0:T(8,128)S(1)} %bitcast.13, f32[3,4096]{1,0:T(4,128)S(1)} %copy-done.1, f32[3,4096]{1,0:T(4,128)S(1)} %copy-done), custom_call_target="tpu_custom_call" | custom-call | flops 20000000000 | bytes 1000000 | tf_op jit(solution)/shard_map/near/pallas_call | solution.py:244
  47.1 2.3 %replies.3 = f32[16,144,128]{2,1,0:T(8,128)} custom-call(s32[16,128]{1,0:T(8,128)S(1)} %bitcast.14, f32[384,128]{1,0:T(8,128)S(1)} %constant_dynamic-update-slice_fusion.refs_1_, f32[384,128]{1,0:T(8,128)S(1)} %collective-permute-done.1.refs_2_, f32[384,128]{1,0:T(8,128)S(1)} %collective-permute-done.2.refs_3_, ...), custom_call_target="tpu_custom_call" | custom-call | tf_op jit(solution)/shard_map/replies/pallas_call | solution.py:370
  49.4 4.5 %all-to-all-done.1 = f32[16,192,128]{2,1,0:T(8,128)S(1)} async-done(((f32[16,192,128]{2,1,0:T(8,128)}), f32[16,192,128]{2,1,0:T(8,128)S(1)}, u32[]{:S(2)}, u32[]{:S(2)}) %all-to-all-start.1) | async-done | bytes 1572896 | tf_op jit(solution)/shard_map/all_to_all | solution.py:363
  53.9 3.7 %all-to-all-start.2 = ((f32[16,144,128]{2,1,0:T(8,128)}), f32[16,144,128]{2,1,0:T(8,128)S(1)}, u32[]{:S(2)}, u32[]{:S(2)}) async-start(f32[16,144,128]{2,1,0:T(8,128)} %replies.3), calls=%async_computation.2 | async-start | bytes 2359296 | tf_op jit(solution)/shard_map/all_to_all | solution.py:363
  57.6 0.0 copy-done.3
  57.6 17.9 %first.1.refs_2_ = f32[3,4096]{1,0:T(4,128)S(1)} custom-call(s32[16,128]{1,0:T(8,128)S(1)} %copy-done.3, f32[3,4096]{1,0:T(4,128)S(1)} %copy-done.1, f32[3,4096]{1,0:T(4,128)S(1)} %near.1.refs_2_.refs_5_, f32[3072,128]{1,0:T(8,128)S(1)} %bitcast.9), custom_call_target="tpu_custom_call" | custom-call | flops 16000000000 | bytes 1000000 | tf_op jit(solution)/shard_map/first/pallas_call | solution.py:244
  75.5 0.0 all-to-all-done.2
  75.5 3.9 %rest.1 = f32[3,4096]{1,0:T(4,128)} custom-call(s32[16,128]{1,0:T(8,128)S(1)} %copy-done.3, f32[3,4096]{1,0:T(4,128)S(1)} %copy-done.1, f32[3,4096]{1,0:T(4,128)S(1)} %first.1.refs_2_, f32[3072,128]{1,0:T(8,128)S(1)} %bitcast.10, f32[2304,128]{1,0:T(8,128)S(1)} %bitcast.11), custom_call_target="tpu_custom_call" | custom-call | flops 6000000000 | bytes 1000000 | tf_op jit(solution)/shard_map/rest/pallas_call | solution.py:244
  (5 shorter events, 0.0 us)
Async XLA Ops:
  2.3 1.5 %collective-permute-start = (f32[192,128]{1,0:T(8,128)}, f32[192,128]{1,0:T(8,128)S(1)}, u32[]{:S(2)}, u32[]{:S(2)}) collective-permute-start(f32[192,128]{1,0:T(8,128)} %get-tuple-element.10), channel_id=1, source_target_pairs={{0,1},{1,0},{2,3},{3,2},{4,5},{5,4},{6,7},{7,6},{8,9},{9,8},{10,11... | collective-permute-start | bytes 294920 | tf_op jit(solution)/shard_map/ppermute | solution.py:366
  3.8 20.1 %collective-permute-start.1 = (f32[384,128]{1,0:T(8,128)S(1)}, f32[384,128]{1,0:T(8,128)S(1)}, u32[]{:S(2)}, u32[]{:S(2)}) collective-permute-start(f32[384,128]{1,0:T(8,128)S(1)} %constant_dynamic-update-slice_fusion.refs_1_), channel_id=1, source_target_pairs={{0,6},{2,0},{4,2},{6,4},{1,7},{3,1},{5,3},{7,5},{8,14},{10,8},{12,... | collective-permute-start | bytes 589832 | tf_op jit(solution)/shard_map/ppermute | solution.py:367
  7.0 17.0 %collective-permute-start.2 = (f32[384,128]{1,0:T(8,128)S(1)}, f32[384,128]{1,0:T(8,128)S(1)}, u32[]{:S(2)}, u32[]{:S(2)}) collective-permute-start(f32[384,128]{1,0:T(8,128)S(1)} %constant_dynamic-update-slice_fusion.refs_1_), channel_id=1, source_target_pairs={{0,4},{2,6},{4,0},{6,2},{1,5},{3,7},{5,1},{7,3},{8,12},{10,14},{12... | collective-permute-start | bytes 589832 | tf_op jit(solution)/shard_map/ppermute | solution.py:367
  7.6 16.3 %collective-permute-start.3 = (f32[384,128]{1,0:T(8,128)S(1)}, f32[384,128]{1,0:T(8,128)S(1)}, u32[]{:S(2)}, u32[]{:S(2)}) collective-permute-start(f32[384,128]{1,0:T(8,128)S(1)} %constant_dynamic-update-slice_fusion.refs_1_), channel_id=1, source_target_pairs={{0,2},{2,4},{4,6},{6,0},{1,3},{3,5},{5,7},{7,1},{8,10},{10,12},{12... | collective-permute-start | bytes 589832 | tf_op jit(solution)/shard_map/ppermute | solution.py:367
  26.5 3.9 %copy-start = (f32[3,4096]{1,0:T(4,128)S(1)}, f32[3,4096]{1,0:T(4,128)}, u32[]{:S(2)}) copy-start(f32[3,4096]{1,0:T(4,128)} %refs_3_.1) | copy-start | bytes 147460
  26.5 3.9 %copy-start.1 = (f32[3,4096]{1,0:T(4,128)S(1)}, f32[3,4096]{1,0:T(4,128)}, u32[]{:S(2)}) copy-start(f32[3,4096]{1,0:T(4,128)} %refs_1_.3) | copy-start | bytes 147460
  26.5 3.9 %copy-start.2 = (s32[32,13]{0,1:T(8,128)S(1)}, s32[32,13]{0,1:T(8,128)}, u32[]{:S(2)}) copy-start(s32[32,13]{0,1:T(8,128)} %param.7) | copy-start | bytes 4996
  26.5 27.4 %all-to-all-start.1 = ((f32[16,192,128]{2,1,0:T(8,128)}), f32[16,192,128]{2,1,0:T(8,128)S(1)}, u32[]{:S(2)}, u32[]{:S(2)}) async-start(f32[16,192,128]{2,1,0:T(8,128)} %replies.2), calls=%async_computation.1 | async-start | bytes 3145728 | tf_op jit(solution)/shard_map/all_to_all | solution.py:363
  49.4 8.3 %copy-start.3 = (s32[16,128]{1,0:T(8,128)S(1)}, s32[16,128]{1,0:T(8,128)}, u32[]{:S(2)}) copy-start(s32[16,128]{1,0:T(8,128)} %get-tuple-element.8.refs_0_) | copy-start | bytes 24580
  53.9 21.6 %all-to-all-start.2 = ((f32[16,144,128]{2,1,0:T(8,128)}), f32[16,144,128]{2,1,0:T(8,128)S(1)}, u32[]{:S(2)}, u32[]{:S(2)}) async-start(f32[16,144,128]{2,1,0:T(8,128)} %replies.3), calls=%async_computation.2 | async-start | bytes 2359296 | tf_op jit(solution)/shard_map/all_to_all | solution.py:363
